TPU v7x, 32 devices: a whole 2x2x4 slice. The times are simulated.
32 devices in a mesh: row: 4 (over x, core), col: 8 (over z, y).
Axes of the slice: x: 2, y: 2, z: 4, core: 2. Of those that a mesh axis runs over, the one named last changes fastest.
Arguments:
- grid_points: int32 [2, 12, 2048], P(None, None, 'row'), may hold values from 0 to 127
- variable: int32 [12, 2048], P(None, 'row'), may hold values from 0 to 2
Outputs:
- panel_factor: float32 [12, 2048, 1536], P(None, ('row', 'col'))
- trailing: float32 [12, 2048, 4096], P(None, 'row', 'col')
All inputs are finite; a program needn't handle non-finite values.
Results may differ from a plain program's by a relative error of at most 0.0042.
Values may be sent and summed in bfloat16 or wider, within the bound.
No kernel may reach another device: no remote copies, remote signals or barrier semaphores. Data moves between devices by JAX's collectives and lax.ppermute only.
A program may use at most 128 MiB of HBM per device.

v0:
```python
import jax
import jax.numpy as jnp
from jax import lax
from jax.sharding import PartitionSpec as P

PANELS = 3
GRID = 128


range_scale = 0.05
nugget = 0.5
rho_first = 0.35
rho_second = 0.2
rho_third = 0.3
highest = lax.Precision.HIGHEST


def kind_scale(kinds):
    return jnp.where(kinds == 0, 1.0, jnp.where(kinds == 1, 1.3, 0.8))


def covariance(row_x, row_y, row_kind, col_x, col_y, col_kind):
    delta_x = (row_x[:, None] - col_x[None, :]).astype(jnp.float32)
    delta_y = (row_y[:, None] - col_y[None, :]).astype(jnp.float32)
    distance = jnp.sqrt(delta_x * delta_x + delta_y * delta_y) * (1.0 / (GRID * range_scale))
    order_sum = row_kind[:, None] + col_kind[None, :]
    dist_square = distance * distance
    dist_cube = dist_square * distance
    dist_fourth = dist_square * dist_square
    polynomial = jnp.where(order_sum == 0, 1.0, 1.0 + distance)
    polynomial = jnp.where(order_sum == 2, 1.0 + distance + dist_square / 3.0, polynomial)
    polynomial = jnp.where(
        order_sum == 3, 1.0 + distance + 0.4 * dist_square + dist_cube / 15.0, polynomial
    )
    polynomial = jnp.where(
        order_sum == 4,
        1.0 + distance + dist_square * (3.0 / 7.0) + dist_cube * (2.0 / 21.0) + dist_fourth / 105.0,
        polynomial,
    )
    correlation = jnp.where(
        row_kind[:, None] == col_kind[None, :],
        1.0,
        jnp.where(order_sum == 1, rho_first, jnp.where(order_sum == 2, rho_second, rho_third)),
    )
    scale_row = kind_scale(row_kind)
    scale_col = kind_scale(col_kind)
    return correlation * scale_row[:, None] * scale_col[None, :] * polynomial * jnp.exp(-distance)


def leading_factor(matrix, count, size):
    remaining = matrix
    lower_blocks = {}
    inverse_blocks = {}
    identity = jnp.eye(size, dtype=jnp.float32)
    for panel_step in range(count):
        row_begin = panel_step * size
        row_end = row_begin + size
        diag_factor = jnp.linalg.cholesky(remaining[row_begin:row_end, row_begin:row_end])
        diag_inverse = lax.linalg.triangular_solve(
            diag_factor, identity, left_side=True, lower=True
        )
        lower_blocks[panel_step, panel_step] = diag_factor
        inverse_blocks[panel_step, panel_step] = diag_inverse
        if panel_step + 1 < count:
            below_rows = jnp.dot(
                remaining[row_end:, row_begin:row_end], diag_inverse.T, precision=highest
            )
            for row_block in range(panel_step + 1, count):
                lower_blocks[row_block, panel_step] = below_rows[
                    (row_block - panel_step - 1) * size : (row_block - panel_step) * size
                ]
            trailing_part = remaining[row_end:, row_end:] - jnp.dot(
                below_rows, below_rows.T, precision=highest
            )
            remaining = remaining.at[row_end:, row_end:].set(trailing_part)
    for row_block in range(count):
        for col_block in range(row_block):
            running = jnp.zeros((size, size), jnp.float32)
            for mid_block in range(col_block, row_block):
                running = running + jnp.dot(
                    lower_blocks[row_block, mid_block],
                    inverse_blocks[mid_block, col_block],
                    precision=highest,
                )
            inverse_blocks[row_block, col_block] = -jnp.dot(
                inverse_blocks[row_block, row_block], running, precision=highest
            )
    zeros_block = jnp.zeros((size, size), jnp.float32)
    lower_rows = []
    inverse_rows = []
    for row_block in range(count):
        lower_rows.append(
            jnp.concatenate(
                [
                    lower_blocks[row_block, col_block] if col_block <= row_block else zeros_block
                    for col_block in range(count)
                ],
                1,
            )
        )
        inverse_rows.append(
            jnp.concatenate(
                [
                    inverse_blocks[row_block, col_block] if col_block <= row_block else zeros_block
                    for col_block in range(count)
                ],
                1,
            )
        )
    return (jnp.concatenate(lower_rows, 0), jnp.concatenate(inverse_rows, 0))


def local(grid_points, variable):
    rows_dev = variable.shape[0]
    tile_size = variable.shape[1]
    row_count = lax.axis_size("row")
    col_count = lax.axis_size("col")
    piece_rows = tile_size // col_count
    row_index = lax.axis_index("row")
    col_index = lax.axis_index("col")
    lead_size = PANELS * tile_size
    all_grid, all_kind = (
        lax.all_gather(grid_points, "row", axis=2, tiled=True),
        lax.all_gather(variable, "row", axis=1, tiled=True),
    )
    coord_x = all_grid[0].reshape(-1)
    coord_y = all_grid[1].reshape(-1)
    kinds = all_kind.reshape(-1)
    lead_x = coord_x[:lead_size]
    lead_y = coord_y[:lead_size]
    lead_kind = kinds[:lead_size]
    lead_cov = covariance(lead_x, lead_y, lead_kind, lead_x, lead_y, lead_kind)
    lead_cov = lead_cov + nugget * jnp.eye(lead_size, dtype=jnp.float32)
    lower_factor, inverse = leading_factor(lead_cov, PANELS, tile_size)
    offset = col_index * piece_rows
    mine_grid = lax.dynamic_slice_in_dim(grid_points, offset, piece_rows, 2)
    mine_kind = lax.dynamic_slice_in_dim(variable, offset, piece_rows, 1)
    piece_cov = covariance(
        mine_grid[0].reshape(-1),
        mine_grid[1].reshape(-1),
        mine_kind.reshape(-1),
        lead_x,
        lead_y,
        lead_kind,
    )
    solved = jnp.dot(piece_cov, inverse.T, precision=highest).reshape(
        rows_dev, piece_rows, lead_size
    )
    lead_rows = lax.dynamic_slice_in_dim(
        lower_factor,
        jnp.minimum(row_index * tile_size + offset, lead_size - piece_rows),
        piece_rows,
        0,
    )
    first_slot = jnp.where(row_index < PANELS, lead_rows, solved[0])
    panel_full = jnp.concatenate([first_slot[None], solved[1:]], 0)
    panel_half = panel_full.astype(jnp.bfloat16)
    target = PANELS + col_index
    col_start = target * tile_size
    col_x = lax.dynamic_slice_in_dim(coord_x, col_start, tile_size)
    col_y = lax.dynamic_slice_in_dim(coord_y, col_start, tile_size)
    col_kind = lax.dynamic_slice_in_dim(kinds, col_start, tile_size)
    row_iota = lax.broadcasted_iota(jnp.int32, (tile_size, tile_size), 0)
    col_iota = lax.broadcasted_iota(jnp.int32, (tile_size, tile_size), 1)

    def assemble(slot):
        cov_block = covariance(
            grid_points[0][slot], grid_points[1][slot], variable[slot], col_x, col_y, col_kind
        )
        equal = (slot * row_count + row_index == target) & (row_iota == col_iota)
        return jnp.where(equal, cov_block + nugget, cov_block)

    cov_tiles = lax.map(assemble, jnp.arange(rows_dev, dtype=jnp.int32))
    target_cov = covariance(col_x, col_y, col_kind, lead_x, lead_y, lead_kind)
    column_rows = jnp.dot(target_cov, inverse.T, precision=highest).astype(jnp.bfloat16)
    update = jnp.einsum(
        "sik,jk->sij",
        lax.all_gather(panel_half, "col", axis=1, tiled=True),
        column_rows,
        preferred_element_type=jnp.float32,
    )
    return (panel_full, cov_tiles - update)


def solution(mesh):
    return jax.shard_map(
        local,
        mesh=mesh,
        in_specs=(P(None, None, "row"), P(None, "row")),
        out_specs=(P(None, ("row", "col"), None), P(None, "row", "col")),
        check_vma=False,
    )
```

profile of v0, /device:TPU:0, one launch (start us, length us, event | category | flops | bytes accessed | tf_op | source)
XLA Modules:
  0.0 1026.9 jit_solution(16386869478165141746)
XLA Ops:
  20.3 18.3 %fusion.28 = f32[1536,1536]{0,1:T(8,128)S(1)} fusion(s32[1536]{0:T(1024)S(1)} %slice.297, s32[1536]{0:T(1024)S(1)} %slice.295, f32[1536]{0:T(1024)S(1)} %select_select_fusion.5, s32[1536]{0:T(1024)S(1)} %slice.293), kind=kLoop, calls=%fused_computation.69 | loop fusion | flops 108527616 | bytes 9461760 | tf_op jit(solution)/shard_map/add | solution.py:133
  44.3 11.7 %cholesky.374 = f32[128,128]{1,0:T(8,128)S(1)} custom-call(f32[128,128]{1,0:T(8,128)S(1)} %cholesky.586), custom_call_target="Cholesky" | custom-call | tf_op jit(solution)/shard_map/jit(cholesky)/cholesky | solution.py:58
  56.2 9.8 custom-call.31
  66.7 11.7 %cholesky.393 = f32[128,128]{1,0:T(8,128)S(1)} custom-call(f32[128,128]{1,0:T(8,128)S(1)} %cholesky.590), custom_call_target="Cholesky" | custom-call | tf_op jit(solution)/shard_map/jit(cholesky)/cholesky | solution.py:58
  78.5 10.0 custom-call.32
  89.1 11.7 %cholesky.414 = f32[128,128]{1,0:T(8,128)S(1)} custom-call(f32[128,128]{1,0:T(8,128)S(1)} %cholesky.595), custom_call_target="Cholesky" | custom-call | tf_op jit(solution)/shard_map/jit(cholesky)/cholesky | solution.py:58
  100.9 9.8 custom-call.33
  111.3 11.7 %cholesky.431 = f32[128,128]{1,0:T(8,128)S(1)} custom-call(f32[128,128]{1,0:T(8,128)S(1)} %convolution_subtract_fusion.19), custom_call_target="Cholesky" | custom-call | tf_op jit(solution)/shard_map/jit(cholesky)/cholesky | solution.py:58
  137.9 39.3 %custom-call.34 = f32[4,128,128]{1,2,0:T(8,128)S(1)} custom-call(f32[4,128,128]{2,1,0:T(8,128)S(1)} %get-tuple-element.206), custom_call_target="InvertDiagBlocksLowerTriangular" | custom-call | tf_op jit(solution)/shard_map/triangular_solve/custom-call.3 | solution.py:59
  204.0 11.7 %cholesky.446 = f32[128,128]{1,0:T(8,128)S(1)} custom-call(f32[128,128]{1,0:T(8,128)S(1)} %cholesky.599), custom_call_target="Cholesky" | custom-call | tf_op jit(solution)/shard_map/jit(cholesky)/cholesky | solution.py:58
  216.4 10.6 %custom-call.35 = f32[1,128,128]{1,2,0:T(8,128)S(1)} custom-call(f32[1,128,128]{2,1,0:T(8,128)} %get-tuple-element.300), custom_call_target="InvertDiagBlocksLowerTriangular" | custom-call | tf_op jit(solution)/shard_map/jit(cholesky)/cholesky | solution.py:58
  234.3 12.5 %cholesky.465 = f32[128,128]{1,0:T(8,128)S(1)} custom-call(f32[128,128]{1,0:T(8,128)} %cholesky.603), custom_call_target="Cholesky" | custom-call | tf_op jit(solution)/shard_map/jit(cholesky)/cholesky | solution.py:58
  250.8 10.2 custom-call.36
  264.9 13.2 %cholesky.486 = f32[128,128]{1,0:T(8,128)} custom-call(f32[128,128]{1,0:T(8,128)} %cholesky.608), custom_call_target="Cholesky" | custom-call | tf_op jit(solution)/shard_map/jit(cholesky)/cholesky | solution.py:58
  280.1 11.3 %custom-call.37 = f32[1,128,128]{1,2,0:T(8,128)} custom-call(f32[1,128,128]{2,1,0:T(8,128)} %get-tuple-element.294), custom_call_target="InvertDiagBlocksLowerTriangular" | custom-call | tf_op jit(solution)/shard_map/jit(cholesky)/cholesky | solution.py:58
  294.5 11.9 %cholesky.503 = f32[128,128]{1,0:T(8,128)S(1)} custom-call(f32[128,128]{1,0:T(8,128)S(1)} %convolution_subtract_fusion.18), custom_call_target="Cholesky" | custom-call | tf_op jit(solution)/shard_map/jit(cholesky)/cholesky | solution.py:58
  317.0 13.3 %while.23 = (s32[]{:T(128)}, f32[512,512]{1,0:T(8,128)}, s32[4,2]{0,1:T(2,128)S(1)}, f32[4,128,128]{2,1,0:T(8,128)}, s32[]{:T(128)}) while((s32[]{:T(128)}, f32[512,512]{1,0:T(8,128)}, s32[4,2]{0,1:T(2,128)S(1)}, f32[4,128,128]{2,1,0:T(8,128)}, s32[]{:T(128)}) %tuple.137), condition=%wide.while_cond.2.clone, body=%wide.while_body.2.clone.sunk | while | flops 2 | bytes 132205 | solution.py:59
  330.3 40.8 %custom-call.38 = f32[4,128,128]{1,2,0:T(8,128)} custom-call(f32[4,128,128]{2,1,0:T(8,128)} %get-tuple-element.207), custom_call_target="InvertDiagBlocksLowerTriangular" | custom-call | tf_op jit(solution)/shard_map/triangular_solve/custom-call.3 | solution.py:59
  390.8 11.7 %cholesky.518 = f32[128,128]{1,0:T(8,128)S(1)} custom-call(f32[128,128]{1,0:T(8,128)S(1)} %cholesky.612), custom_call_target="Cholesky" | custom-call | tf_op jit(solution)/shard_map/jit(cholesky)/cholesky | solution.py:58
  403.2 11.0 %custom-call.39 = f32[1,128,128]{1,2,0:T(8,128)S(1)} custom-call(f32[1,128,128]{2,1,0:T(8,128)} %get-tuple-element.290), custom_call_target="InvertDiagBlocksLowerTriangular" | custom-call | tf_op jit(solution)/shard_map/jit(cholesky)/cholesky | solution.py:58
  433.9 11.7 %cholesky.537 = f32[128,128]{1,0:T(8,128)S(1)} custom-call(f32[128,128]{1,0:T(8,128)S(1)} %slice-done.1), custom_call_target="Cholesky" | custom-call | tf_op jit(solution)/shard_map/jit(cholesky)/cholesky | solution.py:58
  446.3 10.0 custom-call.40
  458.8 11.7 %cholesky.558 = f32[128,128]{1,0:T(8,128)S(1)} custom-call(f32[128,128]{1,0:T(8,128)S(1)} %cholesky.621), custom_call_target="Cholesky" | custom-call | tf_op jit(solution)/shard_map/jit(cholesky)/cholesky | solution.py:58
  470.5 9.8 custom-call.41
  481.8 12.1 %cholesky.575 = f32[128,128]{1,0:T(8,128)S(1)} custom-call(f32[128,128]{1,0:T(8,128)S(1)} %convolution_subtract_fusion.17), custom_call_target="Cholesky" | custom-call | tf_op jit(solution)/shard_map/jit(cholesky)/cholesky | solution.py:58
  502.9 11.8 %while.24 = (s32[]{:T(128)}, f32[512,512]{1,0:T(8,128)}, s32[4,2]{0,1:T(2,128)S(1)}, f32[4,128,128]{2,1,0:T(8,128)S(1)}, s32[]{:T(128)}) while((s32[]{:T(128)}, f32[512,512]{1,0:T(8,128)}, s32[4,2]{0,1:T(2,128)S(1)}, f32[4,128,128]{2,1,0:T(8,128)S(1)}, s32[]{:T(128)}) %tuple.138), condition=%wide.while_cond.2.clone.1, body=%wide.while_body.2.clone.1.sunk | while | flops 2 | bytes 131189 | solution.py:59
  514.7 39.3 %custom-call.42 = f32[4,128,128]{1,2,0:T(8,128)S(1)} custom-call(f32[4,128,128]{2,1,0:T(8,128)S(1)} %get-tuple-element.208), custom_call_target="InvertDiagBlocksLowerTriangular" | custom-call | tf_op jit(solution)/shard_map/triangular_solve/custom-call.3 | solution.py:59
  585.2 39.9 %fusion.47 = f32[768,1536]{1,0:T(8,128)} fusion(f32[512,512]{1,0:T(8,128)S(1)} %cholesky.441, f32[512,512]{1,0:T(8,128)} %pad_maximum_fusion.2, f32[128,512]{1,0:T(8,128)S(1)} %fusion.240, f32[128,512]{1,0:T(8,128)S(1)} %copy-done.26, f32[128,512]{1,0:T(8,128)S(1)} %fusion.243, f32[128,512]{1,0:T(8,128)S(1)} %fusion.212, ...), kind=kOutput, calls=%fused_computation.108 | convolution fusion | flops 21776302080 | bytes 16777216 | tf_op jit(solution)/shard_map/dot_general | solution.py:146
  645.4 33.8 %fusion.116 = bf16[512,1536,1]{1,0,2:T(8,128)(2,1)} fusion(f32[512,512]{1,0:T(8,128)S(1)} %copy-done.24, f32[512,512]{1,0:T(8,128)} %pad_maximum_fusion.2, f32[128,512]{1,0:T(8,128)S(1)} %fusion.240, f32[128,512]{1,0:T(8,128)S(1)} %copy-done.26, f32[128,512]{1,0:T(8,128)S(1)} %fusion.243, f32[128,512]{1,0:T(8,128)S(1)} %fusion.212, ...), kind=kOutput, calls=%fused_computation.177 | convolution fusion | flops 14529331200 | bytes 12058624 | tf_op jit(solution)/shard_map/dot_general | solution.py:175
  679.2 78.8 %while.21 = (s32[]{:T(128)}, f32[12,512,512]{2,1,0:T(8,128)}, s32[12]{0:T(128)S(1)}, s32[]{:T(128)}, s32[]{:T(128)}, /*index=5*/s32[12,512]{1,0:T(8,128)}, s32[5...) while((s32[]{:T(128)}, f32[12,512,512]{2,1,0:T(8,128)}, ...), condition=%wide.region_9.12_spmd.clone, body=%wide.region_8.11_spmd.clone.sunk | while | flops 12324872 | bytes 1183977 | solution.py:173
  758.0 242.8 %all-gather.2.cloned.1.call-done = bf16[12,512,1536]{2,1,0:T(8,128)(2,1)} async-done(((bf16[12,64,1536]{2,1,0:T(8,128)(2,1)}), bf16[12,512,1536]{2,1,0:T(8,128)(2,1)}) %all-gather.2.cloned.1.call-update) | async-done | bytes 18874384 | tf_op jit(solution)/shard_map/all_gather | solution.py:178
  1000.7 19.1 %convolution_subtract_fusion = f32[12,512,512]{2,1,0:T(8,128)} fusion(f32[12,512,512]{2,1,0:T(8,128)} %get-tuple-element.163, bf16[12,512,1536]{2,1,0:T(8,128)(2,1)} %all-gather.2.cloned.1.call-done, bf16[512,1536,1]{1,0,2:T(8,128)(2,1)} %fusion.116), kind=kOutput, calls=%fused_computation.141 | convolution fusion | flops 9666822144 | bytes 45613056 | tf_op jit(solution)/shard_map/sik,jk->sij/dot_general | solution.py:176
  (339 shorter events, 276.5 us)
Async XLA Ops:
  7.2 993.6 %all-gather.2.cloned.1.call-start = ((), (), s32[]{:S(2)}) async-start(), calls=%async_computation | async-start | bytes 21233664 | tf_op jit(solution)/shard_map/all_gather | solution.py:178
  7.3 370.4 %copy-start.3 = (f32[512,512]{1,0:T(8,128)}, f32[512,512]{1,0:T(8,128)S(1)}, u32[]{:S(2)}) copy-start(f32[512,512]{1,0:T(8,128)S(1)} %fusion.177) | copy-start | bytes 3145732
  14.1 6.2 copy-start.42
  14.1 24.6 %copy-start.36 = (s32[1536]{0:T(1024)}, s32[1536]{0:T(1024)S(1)}, u32[]{:S(2)}) copy-start(s32[1536]{0:T(1024)S(1)} %slice.293) | copy-start | bytes 18436
  20.3 18.4 %copy-start.43 = (s32[1,12,2048]{2,0,1:T(1,128)}, s32[1,12,2048]{2,0,1:T(1,128)S(1)}, u32[]{:S(2)}) copy-start(s32[1,12,2048]{2,0,1:T(1,128)S(1)} %get-tuple-element.280) | copy-start | bytes 294916
  20.3 18.4 %copy-start.44 = (s32[1,12,2048]{2,0,1:T(1,128)}, s32[1,12,2048]{2,0,1:T(1,128)S(1)}, u32[]{:S(2)}) copy-start(s32[1,12,2048]{2,0,1:T(1,128)S(1)} %get-tuple-element.279) | copy-start | bytes 294916
  20.3 18.4 %copy-start.38 = (s32[1536]{0:T(1024)}, s32[1536]{0:T(1024)S(1)}, u32[]{:S(2)}) copy-start(s32[1536]{0:T(1024)S(1)} %slice.297) | copy-start | bytes 18436
  20.3 18.4 %copy-start.40 = (s32[1536]{0:T(1024)}, s32[1536]{0:T(1024)S(1)}, u32[]{:S(2)}) copy-start(s32[1536]{0:T(1024)S(1)} %slice.295) | copy-start | bytes 18436
  371.1 9.7 copy-start.2
  372.5 8.2 copy-start.5
  375.0 7.6 copy-start.9
  420.1 8.0 copy-start.8
  420.1 8.0 copy-start.12
  420.1 8.0 copy-start.17
  428.1 5.8 slice-start.1
  431.0 14.7 %copy-start.34 = (f32[384,128]{1,0:T(8,128)S(1)}, f32[384,128]{1,0:T(8,128)}, u32[]{:S(2)}) copy-start(f32[384,128]{1,0:T(8,128)} %copy.31) | copy-start | bytes 589828
  433.9 120.1 %copy-start.4 = (f32[512,512]{1,0:T(8,128)S(1)}, f32[512,512]{1,0:T(8,128)}, u32[]{:S(2)}) copy-start(f32[512,512]{1,0:T(8,128)} %copy-done.3) | copy-start | bytes 3145732
  493.9 6.0 copy-start.13
  500.0 62.9 %copy-start.6 = (f32[128,512]{1,0:T(8,128)S(1)}, f32[128,512]{1,0:T(8,128)}, u32[]{:S(2)}) copy-start(f32[128,512]{1,0:T(8,128)} %copy-done.5) | copy-start | bytes 786436
  500.0 62.9 %copy-start.10 = (f32[128,512]{1,0:T(8,128)S(1)}, f32[128,512]{1,0:T(8,128)}, u32[]{:S(2)}) copy-start(f32[128,512]{1,0:T(8,128)} %copy-done.9) | copy-start | bytes 786436
  500.0 62.9 %copy-start.15 = (f32[128,512]{1,0:T(8,128)S(1)}, f32[128,512]{1,0:T(8,128)}, u32[]{:S(2)}) copy-start(f32[128,512]{1,0:T(8,128)} %copy-done.14) | copy-start | bytes 786436
  554.0 8.9 copy-start.19
  554.1 11.7 %copy-start.18 = (f32[512,512]{1,0:T(8,128)S(1)}, f32[512,512]{1,0:T(8,128)}, u32[]{:S(2)}) copy-start(f32[512,512]{1,0:T(8,128)} %fusion.230) | copy-start | bytes 3145732
  558.6 10.0 copy-start.27
  559.9 10.5 %copy-start.25 = (f32[128,512]{1,0:T(8,128)}, f32[128,512]{1,0:T(8,128)S(1)}, u32[]{:S(2)}) copy-start(f32[128,512]{1,0:T(8,128)S(1)} %fusion.241) | copy-start | bytes 786436
  565.8 8.5 copy-start.33
  565.8 8.8 copy-start.37
  565.8 8.8 copy-start.39
  565.8 8.8 copy-start.41
  570.5 14.7 %copy-start.21 = (f32[128,512]{1,0:T(8,128)S(1)}, f32[128,512]{1,0:T(8,128)}, u32[]{:S(2)}) copy-start(f32[128,512]{1,0:T(8,128)} %copy-done.20) | copy-start | bytes 786436
  573.4 11.8 %copy-start.26 = (f32[128,512]{1,0:T(8,128)S(1)}, f32[128,512]{1,0:T(8,128)}, u32[]{:S(2)}) copy-start(f32[128,512]{1,0:T(8,128)} %copy-done.25) | copy-start | bytes 786436
  636.4 8.9 copy-start.24
  (16 other events, 36.3 us)
Sparse Core Ops, SparseCore 0:
  636.6 364.0 all-gather.1
where the time goes:
time: 1040 us; the launch traced here: 1030 us
  other arithmetic  461 us (44%)
  waiting for transfers between devices  243 us (23%)
  matrix products  173 us (17%)
  local copies, waits for them, and re-layouts  87.8 us (8%)
  loops' own time  26.7 us (3%)
  between operations  23.1 us (2%)
  blocking collectives  12.7 us (1%)
    another operation x44, other arithmetic, leading_factor(): jnp.linalg.cholesky(remaining[row_begin:row_end, row_begin:row_end])  251 us
    all_gather x1, waiting for transfers between devices, local(): lax.all_gather(panel_half, 'col', axis=1, tiled=True)  243 us
    another operation x8, other arithmetic, leading_factor(): lax.linalg.triangular_solve(diag_factor, identity, left_side=True, lower=...  128 us
    dot_general x1, matrix products, local(): jnp.dot(piece_cov, inverse.T, precision=highest)  39.9 us
    dynamic_update_slice x12, other arithmetic, local(): cov_tiles = lax.map(assemble, jnp.arange(rows_dev, dtype=jnp.int32))  36.2 us
    another operation x40, local copies, waits for them, and re-layouts, leading_factor(): lax.linalg.triangular_solve(diag_factor, identity, left_side=True, lower=...  34.2 us
    dot_general x1, matrix products, local(): jnp.dot(target_cov, inverse.T, precision=highest).astype(jnp.bfloat16)  33.8 us
    another operation x1, loops' own time, local(): cov_tiles = lax.map(assemble, jnp.arange(rows_dev, dtype=jnp.int32))  26.5 us
  transfers between devices with their start and end apart: 1, of which 1 were waited for; matrix products, arithmetic and copies ran while one was open for 9% of the time, Pallas kernels for 0%

commit v1 on v0

v1 whole, which is shorter than its diff:
```python
import jax
import jax.numpy as jnp
from jax import lax
from jax.experimental import pallas as pl
from jax.experimental.pallas import tpu as pltpu
from jax.sharding import PartitionSpec as P

PANELS = 3
GRID = 128
SUB = 128
BLOCK = 256
CHUNK = 32

range_scale = 0.05
nugget = 0.5
cross = ((1.0, 0.35, 0.2), (0.35, 1.0, 0.3), (0.2, 0.3, 1.0))
scales = (1.0, 1.3, 0.8)
series = (
    (1.0,),
    (1.0, 1.0),
    (1.0, 1.0, 1.0 / 3.0),
    (1.0, 1.0, 0.4, 1.0 / 15.0),
    (1.0, 1.0, 3.0 / 7.0, 2.0 / 21.0, 1.0 / 105.0),
)
log2e = 1.4426950408889634
step_scale = 1.0 / (GRID * range_scale)
f32 = jnp.float32
bf16 = jnp.bfloat16
NT = (((1,), (1,)), ((), ()))


def column_table(kinds):
    rows = []
    for kind in range(3):
        for power in range(5):
            values = []
            for other in range(3):
                terms = series[kind + other]
                base = cross[kind][other] * scales[kind] * scales[other]
                values.append(base * terms[power] * step_scale**power if power < len(terms) else 0.0)
            rows.append(
                jnp.where(kinds == 0, values[0], jnp.where(kinds == 1, values[1], values[2])).astype(f32)
            )
    rows.append(jnp.zeros_like(rows[0]))
    return jnp.stack(rows, 0)


def dot_nt(left, right):
    return lax.dot_general(left, right, NT, preferred_element_type=f32)


def dot_full(left, right, dims):
    return lax.dot_general(
        left, right, (dims, ((), ())), precision=lax.Precision.HIGHEST, preferred_element_type=f32
    )


def split_two(value):
    high = value.astype(bf16)
    return high, (value - high.astype(f32)).astype(bf16)


def split_three(value):
    high = value.astype(bf16)
    rest = value - high.astype(f32)
    mid = rest.astype(bf16)
    return high, mid, (rest - mid.astype(f32)).astype(bf16)


def covariance(row_x, row_y, row_kind, points, table, lanes):
    width = lanes.size if hasattr(lanes, "size") else lanes.stop - lanes.start
    parts = []
    for piece in range(width // 128):
        at = slice(lanes.start + 128 * piece, lanes.start + 128 * (piece + 1))
        delta_x = row_x - points[0:1, at]
        delta_y = row_y - points[1:2, at]
        square = delta_x * delta_x + delta_y * delta_y
        distance = square * lax.rsqrt(jnp.maximum(square, 1e-6))
        first = row_kind == 0.0
        second = row_kind == 1.0
        total = None
        for power in range(4, -1, -1):
            coef = jnp.where(
                first,
                table[power : power + 1, at],
                jnp.where(second, table[5 + power : 6 + power, at], table[10 + power : 11 + power, at]),
            )
            total = coef if total is None else total * distance + coef
        parts.append(total * jnp.exp2(distance * (-step_scale * log2e)))
    return jnp.concatenate(parts, 1)


def spread_row(value, index):
    return jnp.broadcast_to(value[index : index + 1, :], value.shape)


def spread_lane(value, index):
    return jnp.broadcast_to(value[:, index : index + 1], value.shape)


def inverse_factor(groups):
    count = len(groups)
    shape = groups[0].shape
    lane = lax.broadcasted_iota(jnp.int32, shape, 1)
    sub = lax.broadcasted_iota(jnp.int32, shape, 0)
    result = []
    for block in range(count):
        own = groups[block]
        columns = [spread_lane(own, 8 * block + k) for k in range(8)]
        rows = [spread_row(own, k) for k in range(8)]
        tri = {(j, k): spread_row(columns[k], j) for j in range(8) for k in range(j, 8)}
        inverse = []
        for j in range(8):
            pivot_inverse = 1.0 / tri[j, j]
            inverse.append(pivot_inverse)
            rows[j] = jnp.where(lane == 8 * block + j, tri[j, j] + 1.0, rows[j])
            for k in range(j + 1, 8):
                factor = tri[j, k] * pivot_inverse
                for m in range(k, 8):
                    tri[k, m] = tri[k, m] - factor * tri[j, m]
                rows[k] = rows[k] - factor * rows[j]
        for below in range(block + 1, count):
            column = [spread_lane(groups[below], 8 * block + k) for k in range(8)]
            value = groups[below]
            for j in range(8):
                factor = column[j] * inverse[j]
                for k in range(j + 1, 8):
                    column[k] = column[k] - factor * tri[j, k]
                value = value - factor * rows[j]
            groups[below] = value
        final, pivots = rows[0], inverse[0]
        for j in range(1, 8):
            final = jnp.where(sub == j, rows[j], final)
            pivots = jnp.where(sub == j, inverse[j], pivots)
        root = lax.sqrt(pivots)
        own_lane = 8 * block + sub
        result.append(jnp.where(lane > own_lane, 0.0, jnp.where(lane == own_lane, root, final * root)))
    return result


def kernel(
    place,
    points_rows,
    lead_points,
    lead_table,
    col_points,
    col_table,
    panel_out,
    trail_out,
    matrix,
    row_spread,
    low_high,
    low_rest,
    diag_high,
    diag_mid,
    diag_low,
    sub_inverse,
    sub_lower,
    partial,
    residual,
    rows_high,
    rows_rest,
    col_rows,
):
    step = pl.program_id(0)
    lead = lead_points.shape[1]
    tile = points_rows.shape[2]
    piece = panel_out.shape[1]
    blocks = lead // BLOCK
    row_index = place[0]
    col_index = place[1]
    row_count = place[2]
    target = place[3]

    def spread_points(points, rows):
        turned = points.T
        for which in range(3):
            row_spread[which, 0:rows, :] = jnp.broadcast_to(turned[:, which : which + 1], (rows, 128))

    @pl.when(step == 0)
    def _():
        spread_points(lead_points[...], lead)
        for j in range(blocks):
            lanes = slice(BLOCK * j, BLOCK * (j + 1))

            def fill(index, _, lanes=lanes):
                at = pl.ds(pl.multiple_of(index * CHUNK, CHUNK), CHUNK)
                value = covariance(
                    row_spread[0, at, :],
                    row_spread[1, at, :],
                    row_spread[2, at, :],
                    lead_points,
                    lead_table,
                    lanes,
                )
                row_id = lax.broadcasted_iota(jnp.int32, value.shape, 0) + index * CHUNK
                col_id = lax.broadcasted_iota(jnp.int32, value.shape, 1) + lanes.start
                matrix[at, lanes] = jnp.where(row_id == col_id, value + nugget, value)
                return 0

            lax.fori_loop(BLOCK * j // CHUNK, lead // CHUNK, fill, 0)

        def factor_step(b, _):
            base = pl.multiple_of(b * SUB, SUB)
            here = pl.ds(base, SUB)
            result = inverse_factor([matrix[pl.ds(base + 8 * i, 8), here] for i in range(SUB // 8)])
            half = lax.rem(b, 2)
            for i in range(SUB // 8):
                sub_inverse[half, 8 * i : 8 * i + 8, :] = result[i]

            @pl.when(half == 0)
            def _():
                after = pl.ds(pl.multiple_of(base + SUB, SUB), SUB)
                lower = dot_full(matrix[after, here], sub_inverse[0], ((1,), (1,)))
                sub_lower[...] = lower
                matrix[after, after] = matrix[after, after] - dot_full(lower, lower, ((1,), (1,)))

            @pl.when(half == 1)
            def _():
                t = b // 2
                corner = -dot_full(
                    sub_inverse[1],
                    dot_full(sub_lower[...], sub_inverse[0], ((1,), (0,))),
                    ((1,), (0,)),
                )
                inverse = jnp.concatenate(
                    [
                        jnp.concatenate([sub_inverse[0], jnp.zeros((SUB, SUB), f32)], 1),
                        jnp.concatenate([corner, sub_inverse[1]], 1),
                    ],
                    0,
                )
                high, mid, low = split_three(inverse)
                for copy in range(3):
                    diag_high[t, :, BLOCK * copy : BLOCK * (copy + 1)] = high
                for copy in range(2):
                    diag_mid[t, :, BLOCK * copy : BLOCK * (copy + 1)] = mid
                diag_low[t] = low
                for tt in range(blocks - 1):

                    @pl.when(t == tt)
                    def _(tt=tt):
                        begin = BLOCK * (tt + 1)
                        here = slice(BLOCK * tt, begin)
                        below_high, below_rest = split_two(matrix[begin:, here])
                        solved = (
                            dot_nt(below_high, high) + dot_nt(below_high, mid) + dot_nt(below_rest, high)
                        )
                        solved_high, solved_rest = split_two(solved)
                        low_high[begin:, here] = solved_high
                        low_rest[begin:, here] = solved_rest
                        for j in range(tt + 1, blocks):
                            stripe = slice(BLOCK * j, BLOCK * (j + 1))
                            from_row = BLOCK * j
                            matrix[from_row:, stripe] = matrix[from_row:, stripe] - (
                                dot_nt(low_high[from_row:, here], low_high[stripe, here])
                                + dot_nt(low_high[from_row:, here], low_rest[stripe, here])
                                + dot_nt(low_rest[from_row:, here], low_high[stripe, here])
                            )

            return 0

        lax.fori_loop(0, lead // SUB, factor_step, 0)

    spread_points(points_rows[0], tile)
    row_tile = jnp.where(step == 0, target, (step - 1) * row_count + row_index)
    row_start = row_tile * tile

    def own_diagonal(value, index, col_start):
        row_id = lax.broadcasted_iota(jnp.int32, value.shape, 0) + (row_start + index * CHUNK)
        col_id = lax.broadcasted_iota(jnp.int32, value.shape, 1) + col_start
        return row_id, col_id

    for t in range(blocks):
        lanes = slice(BLOCK * t, BLOCK * (t + 1))
        done = slice(0, BLOCK * t)
        if t:
            partial[:, 0:BLOCK] = (
                dot_nt(rows_high[:, done], low_high[lanes, done])
                + dot_nt(rows_high[:, done], low_rest[lanes, done])
                + dot_nt(rows_rest[:, done], low_high[lanes, done])
            )

        def remain(index, _, t=t, lanes=lanes):
            at = pl.ds(pl.multiple_of(index * CHUNK, CHUNK), CHUNK)
            value = covariance(
                row_spread[0, at, :], row_spread[1, at, :], row_spread[2, at, :], lead_points, lead_table, lanes
            )
            row_id, col_id = own_diagonal(value, index, lanes.start)
            value = jnp.where(row_id == col_id, value + nugget, value)
            if t:
                value = value - partial[at, 0:BLOCK]
            high, mid, low = split_three(value)
            residual[at, 0:BLOCK] = high
            residual[at, BLOCK : 2 * BLOCK] = mid
            residual[at, 2 * BLOCK : 3 * BLOCK] = low
            return 0

        lax.fori_loop(0, tile // CHUNK, remain, 0)
        solved = (
            dot_nt(residual[...], diag_high[t])
            + dot_nt(residual[:, 0 : 2 * BLOCK], diag_mid[t])
            + dot_nt(residual[:, 0:BLOCK], diag_low[t])
        )
        row_id = lax.broadcasted_iota(jnp.int32, solved.shape, 0) + row_start
        col_id = lax.broadcasted_iota(jnp.int32, solved.shape, 1) + lanes.start
        solved = jnp.where(col_id > row_id, 0.0, solved)
        high, rest = split_two(solved)
        rows_high[:, lanes] = high
        rows_rest[:, lanes] = rest

    @pl.when(step == 0)
    def _():
        col_rows[...] = rows_high[...]

    @pl.when(step > 0)
    def _():
        mine = pl.ds(pl.multiple_of(col_index * piece, piece), piece)
        panel_out[0] = rows_high[mine, :].astype(f32) + rows_rest[mine, :].astype(f32)
        partial[...] = dot_nt(rows_high[...], col_rows[...])
        for half in range(tile // BLOCK):
            lanes = slice(BLOCK * half, BLOCK * (half + 1))

            def finish(index, _, lanes=lanes):
                at = pl.ds(pl.multiple_of(index * CHUNK, CHUNK), CHUNK)
                value = covariance(
                    row_spread[0, at, :], row_spread[1, at, :], row_spread[2, at, :], col_points, col_table, lanes
                )
                row_id, col_id = own_diagonal(value, index, target * tile + lanes.start)
                value = jnp.where(row_id == col_id, value + nugget, value)
                trail_out[0, at, lanes] = value - partial[at, lanes]
                return 0

            lax.fori_loop(0, tile // CHUNK, finish, 0)


def local(grid_points, variable):
    slots, tile = variable.shape
    row_count = lax.axis_size("row")
    col_count = lax.axis_size("col")
    piece = tile // col_count
    row_index = lax.axis_index("row")
    col_index = lax.axis_index("col")
    lead = PANELS * tile
    blocks = lead // BLOCK
    used = -(-(PANELS + col_count) // row_count)
    own = jnp.concatenate([grid_points, variable[None]], 0)
    gathered = lax.all_gather(own[:, :used], "row", axis=2, tiled=True).reshape(3, -1)
    target = PANELS + col_index
    pad = lambda value: jnp.pad(value.astype(f32), ((0, 5), (0, 0)))
    lead_points = pad(gathered[:, :lead])
    col_values = lax.dynamic_slice_in_dim(gathered, target * tile, tile, 1)
    col_points = pad(col_values)
    lead_table = column_table(gathered[2, :lead])
    col_table = column_table(col_values[2])
    rows = jnp.concatenate([col_values[:, None], own], 1)
    points_rows = jnp.pad(jnp.transpose(rows, (1, 0, 2)).astype(f32), ((0, 0), (0, 5), (0, 0)))
    place = jnp.stack([row_index, col_index, jnp.int32(row_count), target]).astype(jnp.int32)
    whole = lambda shape: pl.BlockSpec(shape, lambda i, s: (0,) * len(shape))
    flops = 2 * (slots + 1) * tile * lead * lead * 2
    return pl.pallas_call(
        kernel,
        out_shape=(
            jax.ShapeDtypeStruct((slots, piece, lead), f32),
            jax.ShapeDtypeStruct((slots, tile, tile), f32),
        ),
        grid_spec=pltpu.PrefetchScalarGridSpec(
            num_scalar_prefetch=1,
            grid=(slots + 1,),
            in_specs=[
                pl.BlockSpec((1, 8, tile), lambda i, s: (i, 0, 0)),
                whole((8, lead)),
                whole((16, lead)),
                whole((8, tile)),
                whole((16, tile)),
            ],
            out_specs=[
                pl.BlockSpec((1, piece, lead), lambda i, s: (jnp.maximum(i - 1, 0), 0, 0)),
                pl.BlockSpec((1, tile, tile), lambda i, s: (jnp.maximum(i - 1, 0), 0, 0)),
            ],
            scratch_shapes=[
                pltpu.VMEM((lead, lead), f32),
                pltpu.VMEM((3, lead, 128), f32),
                pltpu.VMEM((lead, lead), bf16),
                pltpu.VMEM((lead, lead), bf16),
                pltpu.VMEM((blocks, BLOCK, 3 * BLOCK), bf16),
                pltpu.VMEM((blocks, BLOCK, 2 * BLOCK), bf16),
                pltpu.VMEM((blocks, BLOCK, BLOCK), bf16),
                pltpu.VMEM((2, SUB, SUB), f32),
                pltpu.VMEM((SUB, SUB), f32),
                pltpu.VMEM((tile, tile), f32),
                pltpu.VMEM((tile, 3 * BLOCK), bf16),
                pltpu.VMEM((tile, lead), bf16),
                pltpu.VMEM((tile, lead), bf16),
                pltpu.VMEM((tile, lead), bf16),
            ],
        ),
        compiler_params=pltpu.CompilerParams(
            dimension_semantics=("arbitrary",), vmem_limit_bytes=56 * 1024 * 1024
        ),
        cost_estimate=pl.CostEstimate(
            flops=flops, bytes_accessed=4 * slots * tile * (lead + tile), transcendentals=0
        ),
    )(place, points_rows, lead_points, lead_table, col_points, col_table)


def solution(mesh):
    return jax.shard_map(
        local,
        mesh=mesh,
        in_specs=(P(None, None, "row"), P(None, "row")),
        out_specs=(P(None, ("row", "col"), None), P(None, "row", "col")),
        check_vma=False,
    )
```

time: 1040 us -> 348 us (0.33); the launches traced: 1030 us -> 348 us
  other arithmetic: 461 us -> 2.42 us
  Pallas kernels: 0 us -> 333 us
  waiting for transfers between devices: 243 us -> 0 us
  matrix products: 173 us -> 0 us
  local copies, waits for them, and re-layouts: 87.8 us -> 5.34 us
  loops' own time: 26.7 us -> 0 us
  between operations: 23.1 us -> 0.68 us
    another operation x52 -> x1, other arithmetic: 379 us -> 0.67 us  [local(): jnp.stack([row_index, col_index, jnp.int32(row_count), target])]
    pallas_call x0 -> x1, Pallas kernels: none -> 333 us  [local(): pl.pallas_call(kernel, out_shape=(jax.ShapeDtypeStruct((slots, piece, lea...]
    all_gather x1 -> x0, waiting for transfers between devices: 243 us -> none  [local(): lax.all_gather(panel_half, 'col', axis=1, tiled=True)]
    dot_general x14 -> x0, matrix products: 133 us -> none  [the longest x1 39.9 us: local(): jnp.dot(piece_cov, inverse.T, precision=highest)]
    another operation x58 -> x2, local copies, waits for them, and re-layouts: 43 us -> 2.64 us  [column_table(): return jnp.stack(rows, 0)]
    another operation x39 -> x0, matrix products: 40.2 us -> none  [the longest x21 21.2 us: leading_factor(): lax.linalg.triangular_solve(diag_factor, identity, left_side=True, lower=...]
    dynamic_update_slice x12 -> x0, other arithmetic: 36.2 us -> none  [local(): cov_tiles = lax.map(assemble, jnp.arange(rows_dev, dtype=jnp.int32))]
    another operation x4 -> x0, loops' own time: 26.7 us -> none  [the longest x1 26.5 us: local(): cov_tiles = lax.map(assemble, jnp.arange(rows_dev, dtype=jnp.int32))]
  transfers between devices with their start and end apart: 1 -> 0, of which waited for: 1 -> 0; matrix products, arithmetic and copies ran while one was open for 9% -> 0% of each run, Pallas kernels for 0% -> 0%
where the time goes in v1:
time: 348 us
  Pallas kernels  333 us (96%)
  blocking collectives  6.3 us (2%)
  local copies, waits for them, and re-layouts  5.34 us (2%)
    pallas_call x1, Pallas kernels, local(): pl.pallas_call(kernel, out_shape=(jax.ShapeDtypeStruct((slots, piece, lea...  333 us

profile of v1, /device:TPU:0, one launch (start us, length us, event | category | flops | bytes accessed | tf_op | source)
XLA Modules:
  0.0 347.8 jit_solution(2903824601101214616)
XLA Ops:
  0.6 0.7 pad_add_fusion.1.place
  1.3 0.8 broadcast_in_dim.178
  2.1 0.7 pad_add_fusion
  2.8 6.3 %all_gather.3 = s32[3,3,2048]{2,0,1:T(4,128)S(1)} all-gather(s32[3,3,512]{2,0,1:T(4,128)S(1)} %pad_add_fusion), channel_id=1, replica_groups=mesh['row'=4,'col'=8] {'row'}, dimensions={2}, use_global_device_ids=true | all-gather | bytes 92160 | tf_op jit(solution)/shard_map/all_gather | solution.py:348
  9.1 0.1 select_select_fusion.12
  9.2 0.6 pad.14.col_points
  9.8 1.3 stack.17.col_table
  11.1 0.1 select_select_fusion
  11.2 1.4 stack.16.lead_table
  12.6 0.6 pad.13.lead_points
  13.2 0.8 fusion
  14.0 0.7 pad.12.points_rows
  14.7 333.1 %shard_map.41 = (f32[12,64,1536]{2,1,0:T(8,128)}, f32[12,512,512]{2,1,0:T(8,128)}) custom-call(s32[4]{0:T(128)} %pad_add_fusion.1.place, f32[13,8,512]{2,1,0:T(8,128)} %pad.12.points_rows, f32[8,1536]{1,0:T(8,128)} %pad.13.lead_points, f32[16,1536]{1,0:T(8,128)} %stack.16.lead_table, f32[8,512]{1,0:T(8,128)} %pad.14.col_points, f32[16,512]{1,0:T(8,128)} %stack.17.col_table), custom_call_target="tpu_custom_call" | custom-call | flops 62813896704 | bytes 50331648 | tf_op jit(solution)/shard_map/pallas_call | solution.py:361
  (5 shorter events, 0.0 us)

commit v2 on v1

v2 whole, which is shorter than its diff:
```python
import jax
import jax.numpy as jnp
from jax import lax
from jax.experimental import pallas as pl
from jax.experimental.pallas import tpu as pltpu
from jax.sharding import PartitionSpec as P

PANELS = 3
GRID = 128
SUB = 128
CHUNK = 32

range_scale = 0.05
nugget = 0.5
cross = ((1.0, 0.35, 0.2), (0.35, 1.0, 0.3), (0.2, 0.3, 1.0))
scales = (1.0, 1.3, 0.8)
series = (
    (1.0,),
    (1.0, 1.0),
    (1.0, 1.0, 1.0 / 3.0),
    (1.0, 1.0, 0.4, 1.0 / 15.0),
    (1.0, 1.0, 3.0 / 7.0, 2.0 / 21.0, 1.0 / 105.0),
)
log2e = 1.4426950408889634
step_scale = 1.0 / (GRID * range_scale)
f32 = jnp.float32
bf16 = jnp.bfloat16
NT = (((1,), (1,)), ((), ()))


def column_table(kinds):
    rows = []
    for kind in range(3):
        for power in range(5):
            values = []
            for other in range(3):
                terms = series[kind + other]
                base = cross[kind][other] * scales[kind] * scales[other]
                values.append(base * terms[power] * step_scale**power if power < len(terms) else 0.0)
            rows.append(
                jnp.where(kinds == 0, values[0], jnp.where(kinds == 1, values[1], values[2])).astype(f32)
            )
    rows.append(jnp.zeros_like(rows[0]))
    return jnp.stack(rows, 0)


def dot_nt(left, right):
    return lax.dot_general(left, right, NT, preferred_element_type=f32)


def dot_full(left, right, dims):
    return lax.dot_general(
        left, right, (dims, ((), ())), precision=lax.Precision.HIGHEST, preferred_element_type=f32
    )


def split_two(value):
    high = value.astype(bf16)
    return high, (value - high.astype(f32)).astype(bf16)


def split_three(value):
    high = value.astype(bf16)
    rest = value - high.astype(f32)
    mid = rest.astype(bf16)
    return high, mid, (rest - mid.astype(f32)).astype(bf16)


def covariance(spread, rows, points, table, lanes):
    delta_x = spread[0, rows, :] - points[0:1, lanes]
    delta_y = spread[1, rows, :] - points[1:2, lanes]
    kind = spread[2, rows, :]
    square = delta_x * delta_x + delta_y * delta_y
    distance = square * lax.rsqrt(jnp.maximum(square, 1e-6))
    total = None
    for power in range(4, -1, -1):
        coef = jnp.where(
            kind == 0.0,
            table[power : power + 1, lanes],
            jnp.where(kind == 1.0, table[5 + power : 6 + power, lanes], table[10 + power : 11 + power, lanes]),
        )
        total = coef if total is None else total * distance + coef
    return total * jnp.exp2(distance * (-step_scale * log2e))


def spread_row(value, index):
    return jnp.broadcast_to(value[index : index + 1, :], value.shape)


def spread_lane(value, index):
    return jnp.broadcast_to(value[:, index : index + 1], value.shape)


def inverse_factor(groups):
    count = len(groups)
    shape = groups[0].shape
    lane = lax.broadcasted_iota(jnp.int32, shape, 1)
    sub = lax.broadcasted_iota(jnp.int32, shape, 0)
    result = []
    for block in range(count):
        own = groups[block]
        columns = [spread_lane(own, 8 * block + k) for k in range(8)]
        rows = [spread_row(own, k) for k in range(8)]
        tri = {(j, k): spread_row(columns[k], j) for j in range(8) for k in range(j, 8)}
        inverse = []
        for j in range(8):
            pivot_inverse = 1.0 / tri[j, j]
            inverse.append(pivot_inverse)
            rows[j] = jnp.where(lane == 8 * block + j, tri[j, j] + 1.0, rows[j])
            for k in range(j + 1, 8):
                factor = tri[j, k] * pivot_inverse
                for m in range(k, 8):
                    tri[k, m] = tri[k, m] - factor * tri[j, m]
                rows[k] = rows[k] - factor * rows[j]
        for below in range(block + 1, count):
            column = [spread_lane(groups[below], 8 * block + k) for k in range(8)]
            value = groups[below]
            for j in range(8):
                factor = column[j] * inverse[j]
                for k in range(j + 1, 8):
                    column[k] = column[k] - factor * tri[j, k]
                value = value - factor * rows[j]
            groups[below] = value
        final, pivots = rows[0], inverse[0]
        for j in range(1, 8):
            final = jnp.where(sub == j, rows[j], final)
            pivots = jnp.where(sub == j, inverse[j], pivots)
        root = lax.sqrt(pivots)
        own_lane = 8 * block + sub
        result.append(jnp.where(lane > own_lane, 0.0, jnp.where(lane == own_lane, root, final * root)))
    return result


def kernel(
    place,
    points_rows,
    points_next,
    lead_points,
    lead_table,
    col_points,
    col_table,
    panel_out,
    trail_out,
    matrix,
    row_spread,
    low_pieces,
    diag_first,
    diag_second,
    step_high,
    step_rest,
    sub_inverse,
    sub_lower,
    block_inverse,
    block_lower,
    cov_ahead,
    residual,
    rows_pieces,
    col_rows,
):
    step = pl.program_id(0)
    lead = lead_points.shape[1]
    tile = points_rows.shape[2]
    piece = panel_out.shape[1]
    half_tile = tile // 2
    panels = lead // tile
    blocks = lead // half_tile
    row_index = place[0]
    col_index = place[1]
    row_count = place[2]
    target = place[3]
    chunks = [slice(CHUNK * i, CHUNK * (i + 1)) for i in range(tile // CHUNK)]

    def spread_points(points, rows):
        turned = points.T
        for which in range(3):
            row_spread[which, 0:rows, :] = jnp.broadcast_to(turned[:, which : which + 1], (rows, 128))

    def cov_block(points, table, begin, slot):
        for start in range(0, tile, 128):
            for rows in chunks:
                cov_ahead[slot, rows, start : start + 128] = covariance(
                    row_spread, rows, points, table, slice(begin + start, begin + start + 128)
                )

    def cov_loop(points, table, begin, slot):
        def body(index, _):
            rows = pl.ds(pl.multiple_of(index * 128, 128), 128)
            for start in range(0, tile, 128):
                cov_ahead[slot, rows, start : start + 128] = covariance(
                    row_spread, rows, points, table, slice(begin + start, begin + start + 128)
                )
            return 0

        lax.fori_loop(0, tile // 128, body, 0)

    def add_diagonal(slot):
        for start in range(0, tile, 128):
            here = slice(start, start + 128)
            row_id = lax.broadcasted_iota(jnp.int32, (128, 128), 0)
            col_id = lax.broadcasted_iota(jnp.int32, (128, 128), 1)
            cov_ahead[slot, here, here] = cov_ahead[slot, here, here] + jnp.where(row_id == col_id, nugget, 0.0)

    @pl.when(step == 0)
    def _():
        spread_points(lead_points[...], lead)
        for j in range(blocks):
            begin = half_tile * j

            def fill(index, _, begin=begin):
                at = pl.ds(pl.multiple_of(index * 128, 128), 128)
                for start in range(begin, begin + half_tile, 128):
                    value = covariance(row_spread, at, lead_points, lead_table, slice(start, start + 128))
                    row_id = lax.broadcasted_iota(jnp.int32, value.shape, 0) + index * 128
                    col_id = lax.broadcasted_iota(jnp.int32, value.shape, 1) + start
                    matrix[at, start : start + 128] = jnp.where(row_id == col_id, value + nugget, value)
                return 0

            lax.fori_loop(begin // 128, lead // 128, fill, 0)

        def factor_step(b, _):
            base = pl.multiple_of(b * SUB, SUB)
            here = pl.ds(base, SUB)
            result = inverse_factor([matrix[pl.ds(base + 8 * i, 8), here] for i in range(SUB // 8)])
            half = lax.rem(b, 2)
            for i in range(SUB // 8):
                sub_inverse[half, 8 * i : 8 * i + 8, :] = result[i]

            @pl.when(half == 0)
            def _():
                after = pl.ds(pl.multiple_of(base + SUB, SUB), SUB)
                lower = dot_full(matrix[after, here], sub_inverse[0], ((1,), (1,)))
                sub_lower[...] = lower
                matrix[after, after] = matrix[after, after] - dot_full(lower, lower, ((1,), (1,)))

            @pl.when(half == 1)
            def _():
                block = b // 2
                parity = lax.rem(block, 2)
                corner = -dot_full(
                    sub_inverse[1],
                    dot_full(sub_lower[...], sub_inverse[0], ((1,), (0,))),
                    ((1,), (0,)),
                )
                inverse = jnp.concatenate(
                    [
                        jnp.concatenate([sub_inverse[0], jnp.zeros((SUB, SUB), f32)], 1),
                        jnp.concatenate([corner, sub_inverse[1]], 1),
                    ],
                    0,
                )
                block_inverse[parity] = inverse
                high, mid = split_two(inverse)
                for which in range(blocks):

                    @pl.when(block == which)
                    def _(which=which):
                        begin = half_tile * (which + 1)
                        here = slice(half_tile * which, begin)
                        panel, odd = which // 2, which % 2
                        if begin < lead:
                            below_high, below_rest = split_two(matrix[begin:, here])
                            solved = (
                                dot_nt(below_high, high) + dot_nt(below_high, mid) + dot_nt(below_rest, high)
                            )
                            solved_high, solved_rest = split_two(solved)
                            step_high[begin:, :] = solved_high
                            step_rest[begin:, :] = solved_rest
                            for j in range(which + 1, blocks):
                                stripe = slice(half_tile * j, half_tile * (j + 1))
                                from_row = half_tile * j
                                matrix[from_row:, stripe] = matrix[from_row:, stripe] - (
                                    dot_nt(step_high[from_row:, :], step_high[stripe, :])
                                    + dot_nt(step_high[from_row:, :], step_rest[stripe, :])
                                    + dot_nt(step_rest[from_row:, :], step_high[stripe, :])
                                )
                            later = slice(tile * (panel + 1), lead)
                            if panel + 1 < panels:
                                at = 3 * tile * panel + half_tile * odd
                                low_pieces[later, at : at + half_tile] = step_high[later, :]
                                low_pieces[later, at + tile : at + tile + half_tile] = step_rest[later, :]
                                low_pieces[later, at + 2 * tile : at + 2 * tile + half_tile] = step_high[later, :]
                            if odd == 0:
                                block_lower[...] = solved[0:half_tile, :]
                        if odd == 1:
                            cross_part = -dot_full(
                                block_inverse[1],
                                dot_full(block_lower[...], block_inverse[0], ((1,), (0,))),
                                ((1,), (0,)),
                            )
                            first = split_three(block_inverse[0])
                            second = split_three(cross_part), split_three(block_inverse[1])
                            for order, kind in enumerate((0, 1, 2, 0, 1, 0)):
                                at = slice(half_tile * order, half_tile * (order + 1))
                                diag_first[panel, :, at] = first[kind]
                                for group in range(2):
                                    at = slice(
                                        half_tile * (6 * group + order), half_tile * (6 * group + order + 1)
                                    )
                                    diag_second[panel, :, at] = second[group][kind]

            return 0

        lax.fori_loop(0, lead // SUB, factor_step, 0)
        spread_points(points_rows[0], tile)
        cov_loop(lead_points, lead_table, 0, 0)

    row_tile = jnp.where(step == 0, target, (step - 1) * row_count + row_index)
    always = step >= 0

    for t in range(panels):

        @pl.when(row_tile == t)
        def _(t=t):
            add_diagonal(t % 2)

        @pl.when(always)
        def _(t=t):
            known = None
            if t:
                known = dot_nt(
                    rows_pieces[:, 0 : 3 * tile * t], low_pieces[tile * t : tile * (t + 1), 0 : 3 * tile * t]
                )
            for start in range(0, tile, 128):
                lanes = slice(start, start + 128)
                for rows in chunks:
                    value = cov_ahead[t % 2, rows, lanes]
                    if t:
                        value = value - known[rows, lanes]
                    pieces = split_three(value)
                    at = start if start < half_tile else start + 5 * half_tile
                    for order, kind in enumerate((0, 0, 0, 1, 1, 2)):
                        residual[rows, at + half_tile * order : at + half_tile * order + 128] = pieces[kind]
            for half, diag in enumerate((diag_first, diag_second)):
                solved = dot_nt(residual[:, 0 : 6 * half_tile * (half + 1)], diag[t])
                high, rest = split_two(solved)
                at = 3 * tile * t + half_tile * half
                rows_pieces[:, at : at + half_tile] = high
                if t + 1 < panels:
                    rows_pieces[:, at + tile : at + tile + half_tile] = high
                rows_pieces[:, at + 2 * tile : at + 2 * tile + half_tile] = rest
            if t + 1 < panels:
                cov_block(lead_points, lead_table, tile * (t + 1), (t + 1) % 2)
            else:
                cov_block(col_points, col_table, 0, (t + 1) % 2)

        @pl.when(row_tile <= t)
        def _(t=t):
            for order in (0, 1, 2):
                at = slice(tile * (3 * t + order), tile * (3 * t + order + 1))
                for start in range(0, tile, 128):
                    rows = slice(start, start + 128)
                    value = rows_pieces[rows, at]
                    row_id = lax.broadcasted_iota(jnp.int32, value.shape, 0) + start + row_tile * tile
                    col_id = lax.broadcasted_iota(jnp.int32, value.shape, 1) + t * tile
                    rows_pieces[rows, at] = jnp.where(col_id > row_id, jnp.zeros_like(value), value)

    last = panels % 2

    @pl.when(step == 0)
    def _():
        for t in range(panels):
            col_rows[:, tile * t : tile * (t + 1)] = rows_pieces[:, 3 * tile * t : 3 * tile * t + tile]
        spread_points(points_next[0], tile)
        cov_loop(lead_points, lead_table, 0, 0)

    @pl.when((step > 0) & (row_tile == target))
    def _():
        add_diagonal(last)

    @pl.when(step > 0)
    def _():
        mine = pl.ds(pl.multiple_of(col_index * piece, piece), piece)
        update = None
        for t in range(panels):
            at = 3 * tile * t
            high = rows_pieces[mine, at : at + tile].astype(f32)
            rest = rows_pieces[mine, at + 2 * tile : at + 3 * tile].astype(f32)
            panel_out[0, :, tile * t : tile * (t + 1)] = high + rest
            term = dot_nt(rows_pieces[:, at : at + tile], col_rows[:, tile * t : tile * (t + 1)])
            update = term if update is None else update + term
        for start in range(0, tile, 128):
            lanes = slice(start, start + 128)
            for rows in chunks:
                trail_out[0, rows, lanes] = cov_ahead[last, rows, lanes] - update[rows, lanes]
        spread_points(points_next[0], tile)
        cov_block(lead_points, lead_table, 0, 0)


def local(grid_points, variable):
    slots, tile = variable.shape
    row_count = lax.axis_size("row")
    col_count = lax.axis_size("col")
    piece = tile // col_count
    row_index = lax.axis_index("row")
    col_index = lax.axis_index("col")
    lead = PANELS * tile
    used = -(-(PANELS + col_count) // row_count)
    own = jnp.concatenate([grid_points, variable[None]], 0)
    gathered = lax.all_gather(own[:, :used], "row", axis=2, tiled=True).reshape(3, -1)
    target = PANELS + col_index
    pad = lambda value: jnp.pad(value.astype(f32), ((0, 5), (0, 0)))
    lead_points = pad(gathered[:, :lead])
    col_values = lax.dynamic_slice_in_dim(gathered, target * tile, tile, 1)
    col_points = pad(col_values)
    lead_table = column_table(gathered[2, :lead])
    col_table = column_table(col_values[2])
    rows = jnp.concatenate([col_values[:, None], own], 1)
    points_rows = jnp.pad(jnp.transpose(rows, (1, 0, 2)).astype(f32), ((0, 0), (0, 5), (0, 0)))
    place = jnp.stack([row_index, col_index, jnp.int32(row_count), target]).astype(jnp.int32)
    whole = lambda shape: pl.BlockSpec(shape, lambda i, s: (0,) * len(shape))
    half_tile = tile // 2
    flops = 2 * (slots + 1) * tile * lead * lead * 3
    return pl.pallas_call(
        kernel,
        out_shape=(
            jax.ShapeDtypeStruct((slots, piece, lead), f32),
            jax.ShapeDtypeStruct((slots, tile, tile), f32),
        ),
        grid_spec=pltpu.PrefetchScalarGridSpec(
            num_scalar_prefetch=1,
            grid=(slots + 1,),
            in_specs=[
                pl.BlockSpec((1, 8, tile), lambda i, s: (i, 0, 0)),
                pl.BlockSpec((1, 8, tile), lambda i, s: (jnp.minimum(i + 1, slots), 0, 0)),
                whole((8, lead)),
                whole((16, lead)),
                whole((8, tile)),
                whole((16, tile)),
            ],
            out_specs=[
                pl.BlockSpec((1, piece, lead), lambda i, s: (jnp.maximum(i - 1, 0), 0, 0)),
                pl.BlockSpec((1, tile, tile), lambda i, s: (jnp.maximum(i - 1, 0), 0, 0)),
            ],
            scratch_shapes=[
                pltpu.VMEM((lead, lead), f32),
                pltpu.VMEM((3, lead, 128), f32),
                pltpu.VMEM((lead, 3 * (lead - tile)), bf16),
                pltpu.VMEM((PANELS, half_tile, 6 * half_tile), bf16),
                pltpu.VMEM((PANELS, half_tile, 12 * half_tile), bf16),
                pltpu.VMEM((lead, half_tile), bf16),
                pltpu.VMEM((lead, half_tile), bf16),
                pltpu.VMEM((2, SUB, SUB), f32),
                pltpu.VMEM((SUB, SUB), f32),
                pltpu.VMEM((2, half_tile, half_tile), f32),
                pltpu.VMEM((half_tile, half_tile), f32),
                pltpu.VMEM((2, tile, tile), f32),
                pltpu.VMEM((tile, 12 * half_tile), bf16),
                pltpu.VMEM((tile, 3 * lead), bf16),
                pltpu.VMEM((tile, lead), bf16),
            ],
        ),
        compiler_params=pltpu.CompilerParams(
            dimension_semantics=("arbitrary",), vmem_limit_bytes=58 * 1024 * 1024
        ),
        cost_estimate=pl.CostEstimate(
            flops=flops, bytes_accessed=4 * slots * tile * (lead + tile), transcendentals=0
        ),
    )(place, points_rows, points_rows, lead_points, lead_table, col_points, col_table)


def solution(mesh):
    return jax.shard_map(
        local,
        mesh=mesh,
        in_specs=(P(None, None, "row"), P(None, "row")),
        out_specs=(P(None, ("row", "col"), None), P(None, "row", "col")),
        check_vma=False,
    )
```

time: 348 us -> 261 us (0.75)
  Pallas kernels: 333 us -> 246 us
    pallas_call x1, Pallas kernels: 333 us -> 246 us  [local(): pl.pallas_call(kernel, out_shape=(jax.ShapeDtypeStruct((slots, piece, lea...]
where the time goes in v2:
time: 261 us
  Pallas kernels  246 us (94%)
  blocking collectives  6.3 us (2%)
  local copies, waits for them, and re-layouts  5.34 us (2%)
    pallas_call x1, Pallas kernels, local(): pl.pallas_call(kernel, out_shape=(jax.ShapeDtypeStruct((slots, piece, lea...  246 us
    all_gather x1, blocking collectives, local(): lax.all_gather(own[:, :used], 'row', axis=2, tiled=True).reshape(3, -1)  6.3 us

profile of v2, /device:TPU:0, one launch (start us, length us, event | category | flops | bytes accessed | tf_op | source)
XLA Modules:
  0.0 260.5 jit_solution(6924757009091568700)
XLA Ops:
  0.6 0.7 pad_add_fusion.1.place
  1.3 0.8 broadcast_in_dim.178
  2.1 0.7 pad_add_fusion
  2.8 6.3 %all_gather.3 = s32[3,3,2048]{2,0,1:T(4,128)S(1)} all-gather(s32[3,3,512]{2,0,1:T(4,128)S(1)} %pad_add_fusion), channel_id=1, replica_groups=mesh['row'=4,'col'=8] {'row'}, dimensions={2}, use_global_device_ids=true | all-gather | bytes 92160 | tf_op jit(solution)/shard_map/all_gather | solution.py:399
  9.1 0.1 select_select_fusion.12
  9.2 0.6 pad.14.col_points
  9.8 1.3 stack.17.col_table
  11.1 0.1 select_select_fusion
  11.2 1.4 stack.16.lead_table
  12.6 0.6 pad.13.lead_points
  13.2 0.8 fusion
  14.0 0.7 pad.12.points_rows.points_next
  14.7 245.8 %shard_map.41 = (f32[12,64,1536]{2,1,0:T(8,128)}, f32[12,512,512]{2,1,0:T(8,128)}) custom-call(s32[4]{0:T(128)} %pad_add_fusion.1.place, f32[13,8,512]{2,1,0:T(8,128)} %pad.12.points_rows.points_next, f32[13,8,512]{2,1,0:T(8,128)} %pad.12.points_rows.points_next, f32[8,1536]{1,0:T(8,128)} %pad.13.lead_points, f32[16,1536]{1,0:T(8,128)} %stack.16.lead_table, ...), custom_call_target="tpu_custom_call" | custom-call | flops 94220845056 | bytes 50331648 | tf_op jit(solution)/shard_map/pallas_call | solution.py:413
  (5 shorter events, 0.0 us)

commit v3 on v2

v3 whole, which is shorter than its diff:
```python
import functools
import math

import jax
import jax.numpy as jnp
from jax import lax
from jax.experimental import pallas as pl
from jax.experimental.pallas import tpu as pltpu
from jax.sharding import PartitionSpec as P

PANELS = 3
GRID = 128
SUB = 128
CHUNK = 32
PART = 256
SHARE = 3

range_scale = 0.05
nugget = 0.5
cross = ((1.0, 0.35, 0.2), (0.35, 1.0, 0.3), (0.2, 0.3, 1.0))
scales = (1.0, 1.3, 0.8)
series = (
    (1.0,),
    (1.0, 1.0),
    (1.0, 1.0, 1.0 / 3.0),
    (1.0, 1.0, 0.4, 1.0 / 15.0),
    (1.0, 1.0, 3.0 / 7.0, 2.0 / 21.0, 1.0 / 105.0),
)
log2e = 1.4426950408889634
step_scale = 1.0 / (GRID * range_scale)
f32 = jnp.float32
bf16 = jnp.bfloat16
NT = (((1,), (1,)), ((), ()))


def column_table(kinds):
    rows = []
    for kind in range(3):
        for power in range(5):
            values = []
            for other in range(3):
                terms = series[kind + other]
                base = cross[kind][other] * scales[kind] * scales[other]
                values.append(base * terms[power] * step_scale**power if power < len(terms) else 0.0)
            rows.append(
                jnp.where(kinds == 0, values[0], jnp.where(kinds == 1, values[1], values[2])).astype(f32)
            )
    rows.append(jnp.zeros_like(rows[0]))
    return jnp.stack(rows, 0)


def dot_nt(left, right):
    return lax.dot_general(left, right, NT, preferred_element_type=f32)


def dot_full(left, right, dims):
    return lax.dot_general(
        left, right, (dims, ((), ())), precision=lax.Precision.HIGHEST, preferred_element_type=f32
    )


def split_two(value):
    high = value.astype(bf16)
    return high, (value - high.astype(f32)).astype(bf16)


def split_three(value):
    high = value.astype(bf16)
    rest = value - high.astype(f32)
    mid = rest.astype(bf16)
    return high, mid, (rest - mid.astype(f32)).astype(bf16)


def covariance(spread, rows, points, table, lanes):
    delta_x = spread[0, rows, :] - points[0:1, lanes]
    delta_y = spread[1, rows, :] - points[1:2, lanes]
    kind = spread[2, rows, :]
    square = delta_x * delta_x + delta_y * delta_y
    distance = square * lax.rsqrt(jnp.maximum(square, 1e-6))
    total = None
    for power in range(4, -1, -1):
        coef = jnp.where(
            kind == 0.0,
            table[power : power + 1, lanes],
            jnp.where(kind == 1.0, table[5 + power : 6 + power, lanes], table[10 + power : 11 + power, lanes]),
        )
        total = coef if total is None else total * distance + coef
    return total * jnp.exp2(distance * (-step_scale * log2e))


def spread_row(value, index):
    return jnp.broadcast_to(value[index : index + 1, :], value.shape)


def spread_lane(value, index):
    return jnp.broadcast_to(value[:, index : index + 1], value.shape)


def inverse_factor(groups):
    count = len(groups)
    shape = groups[0].shape
    lane = lax.broadcasted_iota(jnp.int32, shape, 1)
    sub = lax.broadcasted_iota(jnp.int32, shape, 0)
    result = []
    for block in range(count):
        own = groups[block]
        columns = [spread_lane(own, 8 * block + k) for k in range(8)]
        rows = [spread_row(own, k) for k in range(8)]
        tri = {(j, k): spread_row(columns[k], j) for j in range(8) for k in range(j, 8)}
        inverse = []
        for j in range(8):
            if j % 2 == 0:
                second = tri[j, j] * tri[j + 1, j + 1] - tri[j, j + 1] * tri[j, j + 1]
                inverse += [1.0 / tri[j, j], tri[j, j] * (1.0 / second)]
            rows[j] = jnp.where(lane == 8 * block + j, tri[j, j] + 1.0, rows[j])
            for k in range(j + 1, 8):
                factor = tri[j, k] * inverse[j]
                for m in range(k, 8):
                    tri[k, m] = tri[k, m] - factor * tri[j, m]
                rows[k] = rows[k] - factor * rows[j]
        for below in range(block + 1, count):
            column = [spread_lane(groups[below], 8 * block + k) for k in range(8)]
            value = groups[below]
            for j in range(8):
                factor = column[j] * inverse[j]
                for k in range(j + 1, 8):
                    column[k] = column[k] - factor * tri[j, k]
                value = value - factor * rows[j]
            groups[below] = value
        final, pivots = rows[0], inverse[0]
        for j in range(1, 8):
            final = jnp.where(sub == j, rows[j], final)
            pivots = jnp.where(sub == j, inverse[j], pivots)
        root = lax.sqrt(pivots)
        own_lane = 8 * block + sub
        result.append(jnp.where(lane > own_lane, 0.0, jnp.where(lane == own_lane, root, final * root)))
    return result


def spread_points(points, spread):
    rows = points.shape[1]
    turned = points.T
    for which in range(3):
        spread[which, 0:rows, :] = jnp.broadcast_to(turned[:, which : which + 1], (rows, 128))


def covariance_loop(spread, points, table, out, rows_count, width):
    def body(index, _):
        rows = pl.ds(pl.multiple_of(index * 128, 128), 128)
        for start in range(0, width, 128):
            out[rows, start : start + 128] = covariance(spread, rows, points, table, slice(start, start + 128))
        return 0

    lax.fori_loop(0, rows_count // 128, body, 0)


def add_diagonal(block):
    for start in range(0, block.shape[0], 128):
        here = slice(start, start + 128)
        row_id = lax.broadcasted_iota(jnp.int32, (128, 128), 0)
        col_id = lax.broadcasted_iota(jnp.int32, (128, 128), 1)
        block[here, here] = block[here, here] + jnp.where(row_id == col_id, nugget, 0.0)


class Ahead:
    def __init__(self, spread, points, table, begin, out):
        self.args = (spread, points, table, begin, out)
        rows, width = out.shape
        self.units = [
            (start, slice(row, row + CHUNK)) for start in range(0, width, 128) for row in range(0, rows, CHUNK)
        ]
        self.total = len(self.units)

    def share(self, part):
        spread, points, table, begin, out = self.args
        for _ in range(min(len(self.units), math.ceil(self.total * part))):
            start, rows = self.units.pop(0)
            out[rows, start : start + 128] = covariance(
                spread, rows, points, table, slice(begin + start, begin + start + 128)
            )


def row_parts(count):
    return [slice(start, min(start + PART, count)) for start in range(0, count, PART)]


def expand(low, diag, low_pieces, diag_first, diag_second):
    panels, half_tile, _ = diag_first.shape
    tile = 2 * half_tile
    rest_at = low.shape[1] // 2
    for panel in range(panels - 1):
        own = slice(tile * panel, tile * (panel + 1))
        other = slice(rest_at + tile * panel, rest_at + tile * (panel + 1))
        for order, source in enumerate((own, other, own)):
            at = tile * (3 * panel + order)
            low_pieces[tile * panel :, at : at + tile] = low[tile * panel :, source]
    for panel in range(panels):
        for order, kind in enumerate((0, 1, 2, 0, 1, 0)):
            for group in range(3):
                source = slice(half_tile * (3 * group + kind), half_tile * (3 * group + kind + 1))
                place = order if group == 0 else 6 * (group - 1) + order
                at = slice(half_tile * place, half_tile * (place + 1))
                (diag_first if group == 0 else diag_second)[panel, :, at] = diag[panel, :, source]


def solve_block(t, cov, low_pieces, diag_first, diag_second, residual, rows_pieces, ahead):
    panels, half_tile, _ = diag_first.shape
    tile = 2 * half_tile
    parts = row_parts(cov.shape[0])
    portion = 0.25 / len(parts)
    for part in parts:
        known = None
        if t:
            known = dot_nt(rows_pieces[part, 0 : 3 * tile * t], low_pieces[tile * (t - 1) : tile * t, 0 : 3 * tile * t])
        ahead.share(portion)
        for start in range(0, tile, 128):
            lanes = slice(start, start + 128)
            for row in range(part.start, part.stop, CHUNK):
                rows = slice(row, row + CHUNK)
                value = cov[rows, lanes]
                if t:
                    value = value - known[row - part.start : row - part.start + CHUNK, lanes]
                pieces = split_three(value)
                at = start if start < half_tile else start + 5 * half_tile
                for order, kind in enumerate((0, 0, 0, 1, 1, 2)):
                    residual[rows, at + half_tile * order : at + half_tile * order + 128] = pieces[kind]
        ahead.share(portion)
    for part in parts:
        for half, diag in enumerate((diag_first, diag_second)):
            solved = dot_nt(residual[part, 0 : 6 * half_tile * (half + 1)], diag[t])
            ahead.share(portion)
            high, rest = split_two(solved)
            at = 3 * tile * t + half_tile * half
            rows_pieces[part, at : at + half_tile] = high
            if t + 1 < panels:
                rows_pieces[part, at + tile : at + tile + half_tile] = high
            rows_pieces[part, at + 2 * tile : at + 2 * tile + half_tile] = rest
    ahead.share(1.0)


class Nothing:
    def share(self, part):
        pass


def factor_kernel(
    points_rows,
    lead_points,
    lead_table,
    panel_out,
    low,
    diag,
    col_rows,
    shared_rows,
    matrix,
    row_spread,
    low_pieces,
    diag_first,
    diag_second,
    step_high,
    step_rest,
    sub_inverse,
    sub_lower,
    block_inverse,
    block_lower,
    cov_even,
    cov_odd,
    residual,
    rows_pieces,
):
    lead = lead_points.shape[1]
    tile = col_rows.shape[0]
    count = points_rows.shape[1]
    shared, piece, _ = panel_out.shape
    half_tile = tile // 2
    panels = lead // tile
    blocks = lead // half_tile
    rest_at = lead - tile
    spread_points(lead_points[...], row_spread)
    for j in range(blocks):
        begin = half_tile * j

        def fill(index, _, begin=begin):
            at = pl.ds(pl.multiple_of(index * 128, 128), 128)
            for start in range(begin, begin + half_tile, 128):
                value = covariance(row_spread, at, lead_points, lead_table, slice(start, start + 128))
                row_id = lax.broadcasted_iota(jnp.int32, value.shape, 0) + index * 128
                col_id = lax.broadcasted_iota(jnp.int32, value.shape, 1) + start
                matrix[at, start : start + 128] = jnp.where(row_id == col_id, value + nugget, value)
            return 0

        lax.fori_loop(begin // 128, lead // 128, fill, 0)

    def factor_step(b, _):
        base = pl.multiple_of(b * SUB, SUB)
        here = pl.ds(base, SUB)
        result = inverse_factor([matrix[pl.ds(base + 8 * i, 8), here] for i in range(SUB // 8)])
        half = lax.rem(b, 2)
        for i in range(SUB // 8):
            sub_inverse[half, 8 * i : 8 * i + 8, :] = result[i]

        @pl.when(half == 0)
        def _():
            after = pl.ds(pl.multiple_of(base + SUB, SUB), SUB)
            lower = dot_full(matrix[after, here], sub_inverse[0], ((1,), (1,)))
            sub_lower[...] = lower
            matrix[after, after] = matrix[after, after] - dot_full(lower, lower, ((1,), (1,)))

        @pl.when(half == 1)
        def _():
            block = b // 2
            parity = lax.rem(block, 2)
            corner = -dot_full(
                sub_inverse[1],
                dot_full(sub_lower[...], sub_inverse[0], ((1,), (0,))),
                ((1,), (0,)),
            )
            inverse = jnp.concatenate(
                [
                    jnp.concatenate([sub_inverse[0], jnp.zeros((SUB, SUB), f32)], 1),
                    jnp.concatenate([corner, sub_inverse[1]], 1),
                ],
                0,
            )
            block_inverse[parity] = inverse
            high, mid = split_two(inverse)
            for which in range(blocks):

                @pl.when(block == which)
                def _(which=which):
                    begin = half_tile * (which + 1)
                    here = slice(half_tile * which, begin)
                    panel, odd = which // 2, which % 2
                    if begin < lead:
                        below_high, below_rest = split_two(matrix[begin:, here])
                        solved = dot_nt(below_high, high) + dot_nt(below_high, mid) + dot_nt(below_rest, high)
                        solved_high, solved_rest = split_two(solved)
                        step_high[begin:, :] = solved_high
                        step_rest[begin:, :] = solved_rest
                        for j in range(which + 1, blocks):
                            stripe = slice(half_tile * j, half_tile * (j + 1))
                            from_row = half_tile * j
                            matrix[from_row:, stripe] = matrix[from_row:, stripe] - (
                                dot_nt(step_high[from_row:, :], step_high[stripe, :])
                                + dot_nt(step_high[from_row:, :], step_rest[stripe, :])
                                + dot_nt(step_rest[from_row:, :], step_high[stripe, :])
                            )
                        if panel + 1 < panels:
                            later = slice(tile * (panel + 1), lead)
                            target = slice(tile * panel, lead - tile)
                            low[target, here] = step_high[later, :]
                            low[target, rest_at + here.start : rest_at + here.stop] = step_rest[later, :]
                        if odd == 0:
                            block_lower[...] = solved[0:half_tile, :]
                    if odd == 1:
                        cross_part = -dot_full(
                            block_inverse[1],
                            dot_full(block_lower[...], block_inverse[0], ((1,), (0,))),
                            ((1,), (0,)),
                        )
                        for group, value in enumerate((block_inverse[0], cross_part, block_inverse[1])):
                            for kind, part in enumerate(split_three(value)):
                                at = half_tile * (3 * group + kind)
                                diag[panel, :, at : at + half_tile] = part

        return 0

    lax.fori_loop(0, lead // SUB, factor_step, 0)
    expand(low, diag, low_pieces, diag_first, diag_second)
    spread_points(points_rows[...], row_spread)
    covariance_loop(row_spread, lead_points, lead_table, cov_even, count, tile)
    covs = (cov_even, cov_odd)
    always = points_rows[0, 0] >= -1.0
    for t in range(panels):

        @pl.when(always)
        def _(t=t):
            ahead = Nothing()
            if t + 1 < panels:
                ahead = Ahead(row_spread, lead_points, lead_table, tile * (t + 1), covs[(t + 1) % 2])
            solve_block(t, covs[t % 2], low_pieces, diag_first, diag_second, residual, rows_pieces, ahead)

    for t in range(panels):
        at = 3 * tile * t
        lanes = slice(tile * t, tile * (t + 1))
        col_rows[:, lanes] = rows_pieces[0:tile, at : at + tile]
        shared_rows[:, lanes] = rows_pieces[tile : tile + shared * piece, at : at + tile]
        for slot in range(shared):
            rows = slice(tile + piece * slot, tile + piece * (slot + 1))
            panel_out[slot, :, lanes] = rows_pieces[rows, at : at + tile].astype(f32) + rows_pieces[
                rows, at + 2 * tile : at + 3 * tile
            ].astype(f32)


def rows_kernel(
    place,
    points_rows,
    points_next,
    lead_points,
    lead_table,
    col_points,
    col_table,
    low,
    diag,
    col_rows,
    panel_in,
    panel_out,
    trail_out,
    row_spread,
    low_pieces,
    diag_first,
    diag_second,
    cov_even,
    cov_odd,
    residual,
    rows_pieces,
):
    step = pl.program_id(0)
    tile = points_rows.shape[2]
    piece = panel_out.shape[1]
    panels = lead_points.shape[1] // tile
    row_index, col_index, row_count, target = place[0], place[1], place[2], place[3]
    row_tile = step * row_count + row_index
    covs = (cov_even, cov_odd)

    @pl.when(step == 0)
    def _():
        expand(low, diag, low_pieces, diag_first, diag_second)
        spread_points(points_rows[0], row_spread)
        covariance_loop(row_spread, lead_points, lead_table, cov_even, tile, tile)

    for t in range(panels):

        @pl.when(row_tile == t)
        def _(t=t):
            add_diagonal(covs[t % 2])

        @pl.when(step >= 0)
        def _(t=t):
            if t + 1 < panels:
                ahead = Ahead(row_spread, lead_points, lead_table, tile * (t + 1), covs[(t + 1) % 2])
            else:
                ahead = Ahead(row_spread, col_points, col_table, 0, covs[(t + 1) % 2])
            solve_block(t, covs[t % 2], low_pieces, diag_first, diag_second, residual, rows_pieces, ahead)

        @pl.when(row_tile <= t)
        def _(t=t):
            for order in (0, 1, 2):
                at = slice(tile * (3 * t + order), tile * (3 * t + order + 1))
                for start in range(0, tile, 128):
                    rows = slice(start, start + 128)
                    value = rows_pieces[rows, at]
                    row_id = lax.broadcasted_iota(jnp.int32, value.shape, 0) + start + row_tile * tile
                    col_id = lax.broadcasted_iota(jnp.int32, value.shape, 1) + t * tile
                    rows_pieces[rows, at] = jnp.where(col_id > row_id, jnp.zeros_like(value), value)

    last = covs[panels % 2]

    @pl.when(row_tile == target)
    def _():
        add_diagonal(last)

    @pl.when(step >= 0)
    def _():
        spread_points(points_next[0], row_spread)
        mine = pl.ds(pl.multiple_of(col_index * piece, piece), piece)
        ahead = Ahead(row_spread, lead_points, lead_table, 0, covs[0])
        for t in range(panels):
            at = 3 * tile * t
            high = rows_pieces[mine, at : at + tile].astype(f32)
            rest = rows_pieces[mine, at + 2 * tile : at + 3 * tile].astype(f32)
            panel_out[0, :, tile * t : tile * (t + 1)] = high + rest
        parts = row_parts(tile)
        for part in parts:
            update = None
            for t in range(panels):
                at = 3 * tile * t
                term = dot_nt(rows_pieces[part, at : at + tile], col_rows[:, tile * t : tile * (t + 1)])
                update = term if update is None else update + term
            ahead.share(0.5 / len(parts))
            trail_out[0, part, :] = last[part, :] - update
            ahead.share(0.5 / len(parts))
        ahead.share(1.0)


def trail_kernel(first, place, points_rows, col_points, col_table, rows, col_rows, trail_in, trail_out, row_spread):
    tile = points_rows.shape[2]
    spread_points(points_rows[0], row_spread)
    row_tile = (first + pl.program_id(0)) * place[2] + place[0]
    for part in row_parts(tile):
        update = dot_nt(rows[0, part, :], col_rows[...])
        for start in range(0, tile, 128):
            lanes = slice(start, start + 128)
            for row in range(part.start, part.stop, CHUNK):
                value = covariance(row_spread, slice(row, row + CHUNK), col_points, col_table, lanes)
                trail_out[0, row : row + CHUNK, lanes] = (
                    value - update[row - part.start : row - part.start + CHUNK, lanes]
                )

    @pl.when(row_tile == place[3])
    def _():
        add_diagonal(trail_out.at[0])


def local(grid_points, variable):
    slots, tile = variable.shape
    row_count = lax.axis_size("row")
    col_count = lax.axis_size("col")
    piece = tile // col_count
    row_index = lax.axis_index("row")
    col_index = lax.axis_index("col")
    lead = PANELS * tile
    half_tile = tile // 2
    shared = slots // SHARE
    kept = slots - shared
    used = -(-(PANELS + col_count) // row_count)
    own = jnp.concatenate([grid_points, variable[None]], 0)
    gathered = lax.all_gather(own[:, :used], "row", axis=2, tiled=True).reshape(3, -1)
    target = PANELS + col_index
    pad = lambda value: jnp.pad(value.astype(f32), ((0, 5), (0, 0)))
    lead_points = pad(gathered[:, :lead])
    col_values = lax.dynamic_slice_in_dim(gathered, target * tile, tile, 1)
    col_points = pad(col_values)
    lead_table = column_table(gathered[2, :lead])
    col_table = column_table(col_values[2])
    points_rows = jnp.pad(jnp.transpose(own, (1, 0, 2)).astype(f32), ((0, 0), (0, 5), (0, 0)))
    pieces = lax.dynamic_slice_in_dim(own[:, kept:], col_index * piece, piece, 2).reshape(3, shared * piece)
    first_rows = jnp.concatenate([col_values, pieces], 1).astype(f32)
    count = -(-first_rows.shape[1] // 128) * 128
    first_rows = jnp.pad(first_rows, ((0, 5), (0, count - first_rows.shape[1])))
    place = jnp.stack([row_index, col_index, jnp.int32(row_count), target]).astype(jnp.int32)
    whole = lambda shape: pl.BlockSpec(shape, lambda i, *s: (0,) * len(shape))
    panel_shape = jax.ShapeDtypeStruct((slots, piece, lead), f32)
    trail_shape = jax.ShapeDtypeStruct((slots, tile, tile), f32)
    low_shape = (lead - tile, 2 * (lead - tile))
    diag_shape = (PANELS, half_tile, 9 * half_tile)
    layout = [
        pltpu.VMEM((lead - tile, 3 * (lead - tile)), bf16),
        pltpu.VMEM((PANELS, half_tile, 6 * half_tile), bf16),
        pltpu.VMEM((PANELS, half_tile, 12 * half_tile), bf16),
    ]
    buffers = lambda rows: [
        pltpu.VMEM((rows, tile), f32),
        pltpu.VMEM((rows, tile), f32),
        pltpu.VMEM((rows, 12 * half_tile), bf16),
        pltpu.VMEM((rows, 3 * lead), bf16),
    ]
    params = pltpu.CompilerParams(dimension_semantics=("arbitrary",), vmem_limit_bytes=58 * 1024 * 1024)
    cost = lambda rows, size: pl.CostEstimate(flops=6 * rows * lead * lead, bytes_accessed=size, transcendentals=0)
    panel, low, diag, col_rows, shared_rows = pl.pallas_call(
        factor_kernel,
        out_shape=(
            panel_shape,
            jax.ShapeDtypeStruct(low_shape, bf16),
            jax.ShapeDtypeStruct(diag_shape, bf16),
            jax.ShapeDtypeStruct((tile, lead), bf16),
            jax.ShapeDtypeStruct((shared * piece, lead), bf16),
        ),
        grid=(1,),
        in_specs=[whole((8, count)), whole((8, lead)), whole((16, lead))],
        out_specs=(
            pl.BlockSpec((shared, piece, lead), lambda i: (SHARE - 1, 0, 0)),
            whole(low_shape),
            whole(diag_shape),
            whole((tile, lead)),
            whole((shared * piece, lead)),
        ),
        scratch_shapes=[pltpu.VMEM((lead, lead), f32), pltpu.VMEM((3, lead, 128), f32)]
        + layout
        + [
            pltpu.VMEM((lead, half_tile), bf16),
            pltpu.VMEM((lead, half_tile), bf16),
            pltpu.VMEM((2, SUB, SUB), f32),
            pltpu.VMEM((SUB, SUB), f32),
            pltpu.VMEM((2, half_tile, half_tile), f32),
            pltpu.VMEM((half_tile, half_tile), f32),
        ]
        + buffers(count),
        compiler_params=params,
        cost_estimate=cost(count + lead, 20 * tile * lead),
    )(first_rows, lead_points, lead_table)
    panel_half = lax.all_gather(shared_rows.reshape(shared, piece, lead), "col", axis=1, tiled=True)
    panel, trail = pl.pallas_call(
        rows_kernel,
        out_shape=(panel_shape, trail_shape),
        grid_spec=pltpu.PrefetchScalarGridSpec(
            num_scalar_prefetch=1,
            grid=(kept,),
            in_specs=[
                pl.BlockSpec((1, 8, tile), lambda i, s: (i, 0, 0)),
                pl.BlockSpec((1, 8, tile), lambda i, s: (jnp.minimum(i + 1, kept - 1), 0, 0)),
                whole((8, lead)),
                whole((16, lead)),
                whole((8, tile)),
                whole((16, tile)),
                whole(low_shape),
                whole(diag_shape),
                whole((tile, lead)),
                pl.BlockSpec(memory_space=pl.ANY),
            ],
            out_specs=[
                pl.BlockSpec((1, piece, lead), lambda i, s: (i, 0, 0)),
                pl.BlockSpec((1, tile, tile), lambda i, s: (i, 0, 0)),
            ],
            scratch_shapes=[pltpu.VMEM((3, tile, 128), f32)] + layout + buffers(tile),
        ),
        input_output_aliases={10: 0},
        compiler_params=params,
        cost_estimate=cost(kept * tile, 4 * kept * tile * (lead + tile)),
    )(place, points_rows, points_rows, lead_points, lead_table, col_points, col_table, low, diag, col_rows, panel)
    trail = pl.pallas_call(
        functools.partial(trail_kernel, kept),
        out_shape=trail_shape,
        grid_spec=pltpu.PrefetchScalarGridSpec(
            num_scalar_prefetch=1,
            grid=(shared,),
            in_specs=[
                pl.BlockSpec((1, 8, tile), lambda i, s: (kept + i, 0, 0)),
                whole((8, tile)),
                whole((16, tile)),
                pl.BlockSpec((1, tile, lead), lambda i, s: (i, 0, 0)),
                whole((tile, lead)),
                pl.BlockSpec(memory_space=pl.ANY),
            ],
            out_specs=pl.BlockSpec((1, tile, tile), lambda i, s: (kept + i, 0, 0)),
            scratch_shapes=[pltpu.VMEM((3, tile, 128), f32)],
        ),
        input_output_aliases={6: 0},
        compiler_params=params,
        cost_estimate=cost(shared * tile // 3, 4 * shared * tile * (lead + tile)),
    )(place, points_rows, col_points, col_table, panel_half, col_rows, trail)
    return panel, trail


def solution(mesh):
    return jax.shard_map(
        local,
        mesh=mesh,
        in_specs=(P(None, None, "row"), P(None, "row")),
        out_specs=(P(None, ("row", "col"), None), P(None, "row", "col")),
        check_vma=False,
    )
```

time: 261 us -> 234 us (0.90); the launches traced: 261 us -> 231 us
  Pallas kernels: 246 us -> 202 us
  between operations: 0.68 us -> 14.3 us
    pallas_call x1 -> x3, Pallas kernels: 246 us -> 202 us  [the longest x1 103 us: local(): pl.pallas_call(rows_kernel, out_shape=(panel_shape, trail_shape), grid_sp...]
  transfers between devices with their start and end apart: 0 -> 1, of which waited for: 0 -> 0; matrix products, arithmetic and copies ran while one was open for 0% -> 1% of each run, Pallas kernels for 0% -> 45%
where the time goes in v3:
time: 234 us; the launch traced here: 231 us
  Pallas kernels  202 us (86%)
  between operations  14.3 us (6%)
  local copies, waits for them, and re-layouts  6.82 us (3%)
  blocking collectives  6.3 us (3%)
    pallas_call x1, Pallas kernels, local(): pl.pallas_call(rows_kernel, out_shape=(panel_shape, trail_shape), grid_sp...  103 us
    pallas_call x1, Pallas kernels, local(): pl.pallas_call(factor_kernel, out_shape=(panel_shape, jax.ShapeDtypeStruc...  88.4 us
    pallas_call x1, Pallas kernels, local(): pl.pallas_call(functools.partial(trail_kernel, kept), out_shape=trail_sha...  10.4 us
    all_gather x1, blocking collectives, local(): lax.all_gather(own[:, :used], 'row', axis=2, tiled=True).reshape(3, -1)  6.3 us
  transfers between devices with their start and end apart: 1, of which 0 were waited for; matrix products, arithmetic and copies ran while one was open for 1% of the time, Pallas kernels for 45%

profile of v3, /device:TPU:0, one launch (start us, length us, event | category | flops | bytes accessed | tf_op | source)
XLA Modules:
  0.0 230.8 jit_solution(8856522011045426427)
XLA Ops:
  7.2 0.0 all-gather.2.cloned.1.call-start
  7.2 0.8 broadcast_in_dim.175
  8.0 0.7 fusion.2
  8.7 6.3 %all_gather.6 = s32[3,3,2048]{2,0,1:T(4,128)S(1)} all-gather(s32[3,3,512]{2,0,1:T(4,128)S(1)} %fusion.2), channel_id=1, replica_groups=mesh['row'=4,'col'=8] {'row'}, dimensions={2}, use_global_device_ids=true | all-gather | bytes 92160 | tf_op jit(solution)/shard_map/all_gather | solution.py:518
  15.0 0.1 select_select_fusion
  15.1 0.7 pad_slice_fusion
  15.9 0.1 dynamic-slice_add_fusion
  16.0 0.1 reshape.14
  16.0 0.6 pad.17.lead_points
  16.7 0.6 pad.19.points_rows
  17.3 1.4 stack.16.lead_table
  18.7 0.0 copy-start
  18.7 88.4 %shard_map.41 = (f32[12,64,1536]{2,1,0:T(8,128)}, bf16[1024,2048]{1,0:T(8,128)(2,1)}, bf16[3,256,2304]{2,1,0:T(8,128)(2,1)}, bf16[512,1536]{1,0:T(8,128)(2,1)}, bf16[256,1536]{1,0:T(8,128)(2,1)}) custom-call(f32[8,768]{1,0:T(8,128)} %pad.19.points_rows, f32[8,1536]{1,0:T(8,128)} %pad.17.lead_points, f32[16,1536]{1,0:T(8,128)} %stack.16.lead_table), custom_call_target="tpu_custom_call" | custom-call | flops 32614907904 | bytes 15728640 | tf_op jit(solution)/shard_map/pallas_call | solution.py:550
  107.1 0.0 all-gather.2.cloned.1.call-update
  107.1 0.0 copy-done
  107.2 0.7 pad.16.points_rows.points_next
  107.9 0.6 pad.18.col_points
  108.5 0.1 select_select_fusion.12
  108.6 1.3 stack.17.col_table
  109.9 0.7 pad_add_fusion.1.place
  110.5 102.9 %shard_map.42 = (f32[12,64,1536]{2,1,0:T(8,128)}, f32[12,512,512]{2,1,0:T(8,128)}) custom-call(s32[4]{0:T(128)} %pad_add_fusion.1.place, f32[12,8,512]{2,1,0:T(8,128)} %pad.16.points_rows.points_next, f32[12,8,512]{2,1,0:T(8,128)} %pad.16.points_rows.points_next, f32[8,1536]{1,0:T(8,128)} %pad.17.lead_points, ...), custom_call_target="tpu_custom_call", output_to_operand_aliasing={{0}: (10, {})} | custom-call | flops 57982058496 | bytes 33554432 | tf_op jit(solution)/shard_map/pallas_call | solution.py:583
  213.4 0.0 all-gather.2.cloned.1.call-done.rows
  213.4 10.4 %shard_map.43 = f32[12,512,512]{2,1,0:T(8,128)} custom-call(s32[4]{0:T(128)} %pad_add_fusion.1.place, f32[12,8,512]{2,1,0:T(8,128)} %pad.16.points_rows.points_next, f32[8,512]{1,0:T(8,128)} %pad.18.col_points, f32[16,512]{1,0:T(8,128)} %stack.17.col_table, bf16[4,512,1536]{2,1,0:T(8,128)(2,1)} %all-gather.2.cloned.1.call-done.rows, ...), custom_call_target="tpu_custom_call", output_to_operand_aliasing={{}: (6, {})} | custom-call | flops 9654239232 | bytes 16777216 | tf_op jit(solution)/shard_map/pallas_call | solution.py:611
  (8 shorter events, 0.1 us)
Async XLA Ops:
  7.2 206.2 %all-gather.2.cloned.1.call-start = ((), (), s32[]{:S(2)}) async-start(), calls=%async_computation | async-start | bytes 7077888 | tf_op jit(solution)/shard_map/all_gather | solution.py:582
  18.7 88.5 %copy-start = (s32[2,12,512]{2,0,1:T(2,128)S(1)}, s32[2,12,512]{2,0,1:T(2,128)}, u32[]{:S(2)}) copy-start(s32[2,12,512]{2,0,1:T(2,128)} %param.2) | copy-start | bytes 147460
Sparse Core Ops, SparseCore 0:
  107.2 100.7 all-gather.1

commit v4 on v3

--- a/solution.py
+++ b/solution.py
@@ -13,7 +13,8 @@
 SUB = 128
 CHUNK = 32
 PART = 256
-SHARE = 3
+GROUP = 4
+SHARED, SLOTS = 5, 12
 
 range_scale = 0.05
 nugget = 0.5
@@ -33,8 +34,8 @@
 NT = (((1,), (1,)), ((), ()))
 
 
-def column_table(kinds):
-    rows = []
+def column_table(points, table):
+    kinds = points[2:3, :]
     for kind in range(3):
         for power in range(5):
             values = []
@@ -42,11 +43,10 @@
                 terms = series[kind + other]
                 base = cross[kind][other] * scales[kind] * scales[other]
                 values.append(base * terms[power] * step_scale**power if power < len(terms) else 0.0)
-            rows.append(
-                jnp.where(kinds == 0, values[0], jnp.where(kinds == 1, values[1], values[2])).astype(f32)
+            at = 5 * kind + power
+            table[at : at + 1, :] = jnp.where(
+                kinds == 0.0, values[0], jnp.where(kinds == 1.0, values[1], values[2])
             )
-    rows.append(jnp.zeros_like(rows[0]))
-    return jnp.stack(rows, 0)
 
 
 def dot_nt(left, right):
@@ -139,9 +139,19 @@
 
 def spread_points(points, spread):
     rows = points.shape[1]
-    turned = points.T
+    turned = points[...].T
     for which in range(3):
         spread[which, 0:rows, :] = jnp.broadcast_to(turned[:, which : which + 1], (rows, 128))
+
+
+def take_slot(own, slot, points):
+    for which in range(3):
+        points[which : which + 1, :] = own[which, pl.ds(slot, 1), :].astype(f32)
+
+
+def take_columns(gathered, begin, points):
+    for which in range(3):
+        points[which : which + 1, :] = gathered[which : which + 1, pl.ds(begin, points.shape[1])].astype(f32)
 
 
 def covariance_loop(spread, points, table, out, rows_count, width):
@@ -244,14 +254,17 @@
 
 
 def factor_kernel(
-    points_rows,
-    lead_points,
-    lead_table,
+    place,
+    first_rows,
+    gathered,
     panel_out,
     low,
     diag,
     col_rows,
     shared_rows,
+    row_points,
+    lead_points,
+    lead_table,
     matrix,
     row_spread,
     low_pieces,
@@ -263,20 +276,20 @@
     sub_lower,
     block_inverse,
     block_lower,
-    cov_even,
-    cov_odd,
     residual,
     rows_pieces,
 ):
     lead = lead_points.shape[1]
     tile = col_rows.shape[0]
-    count = points_rows.shape[1]
+    count = first_rows.shape[1]
     shared, piece, _ = panel_out.shape
     half_tile = tile // 2
     panels = lead // tile
     blocks = lead // half_tile
     rest_at = lead - tile
-    spread_points(lead_points[...], row_spread)
+    take_columns(gathered, 0, lead_points)
+    column_table(lead_points, lead_table)
+    spread_points(lead_points, row_spread)
     for j in range(blocks):
         begin = half_tile * j
 
@@ -367,10 +380,11 @@
 
     lax.fori_loop(0, lead // SUB, factor_step, 0)
     expand(low, diag, low_pieces, diag_first, diag_second)
-    spread_points(points_rows[...], row_spread)
-    covariance_loop(row_spread, lead_points, lead_table, cov_even, count, tile)
-    covs = (cov_even, cov_odd)
-    always = points_rows[0, 0] >= -1.0
+    row_points[0:3, :] = first_rows[...].astype(f32)
+    spread_points(row_points, row_spread)
+    covs = tuple(matrix.at[0:count, begin : begin + tile] for begin in (0, tile))
+    covariance_loop(row_spread, lead_points, lead_table, covs[0], count, tile)
+    always = place[0] >= 0
     for t in range(panels):
 
         @pl.when(always)
@@ -384,9 +398,10 @@
         at = 3 * tile * t
         lanes = slice(tile * t, tile * (t + 1))
         col_rows[:, lanes] = rows_pieces[0:tile, at : at + tile]
-        shared_rows[:, lanes] = rows_pieces[tile : tile + shared * piece, at : at + tile]
+        shared_rows[:, lanes] = rows_pieces[tile : tile + shared_rows.shape[0], at : at + tile]
         for slot in range(shared):
-            rows = slice(tile + piece * slot, tile + piece * (slot + 1))
+            begin = tile + shared_rows.shape[0] // shared * slot + place[1] // GROUP * piece
+            rows = pl.ds(pl.multiple_of(begin, piece), piece)
             panel_out[slot, :, lanes] = rows_pieces[rows, at : at + tile].astype(f32) + rows_pieces[
                 rows, at + 2 * tile : at + 3 * tile
             ].astype(f32)
@@ -394,18 +409,18 @@
 
 def rows_kernel(
     place,
-    points_rows,
-    points_next,
+    own,
+    gathered,
+    low,
+    diag,
+    col_rows,
+    panel_out,
+    trail_out,
+    row_points,
     lead_points,
     lead_table,
     col_points,
     col_table,
-    low,
-    diag,
-    col_rows,
-    panel_in,
-    panel_out,
-    trail_out,
     row_spread,
     low_pieces,
     diag_first,
@@ -416,7 +431,7 @@
     rows_pieces,
 ):
     step = pl.program_id(0)
-    tile = points_rows.shape[2]
+    tile = row_points.shape[1]
     piece = panel_out.shape[1]
     panels = lead_points.shape[1] // tile
     row_index, col_index, row_count, target = place[0], place[1], place[2], place[3]
@@ -426,7 +441,12 @@
     @pl.when(step == 0)
     def _():
         expand(low, diag, low_pieces, diag_first, diag_second)
-        spread_points(points_rows[0], row_spread)
+        take_columns(gathered, 0, lead_points)
+        column_table(lead_points, lead_table)
+        take_columns(gathered, pl.multiple_of(target * tile, tile), col_points)
+        column_table(col_points, col_table)
+        take_slot(own, 0, row_points)
+        spread_points(row_points, row_spread)
         covariance_loop(row_spread, lead_points, lead_table, cov_even, tile, tile)
 
     for t in range(panels):
@@ -462,7 +482,8 @@
 
     @pl.when(step >= 0)
     def _():
-        spread_points(points_next[0], row_spread)
+        take_slot(own, jnp.minimum(step + 1, pl.num_programs(0) - 1), row_points)
+        spread_points(row_points, row_spread)
         mine = pl.ds(pl.multiple_of(col_index * piece, piece), piece)
         ahead = Ahead(row_spread, lead_points, lead_table, 0, covs[0])
         for t in range(panels):
@@ -483,12 +504,47 @@
         ahead.share(1.0)
 
 
-def trail_kernel(first, place, points_rows, col_points, col_table, rows, col_rows, trail_in, trail_out, row_spread):
-    tile = points_rows.shape[2]
-    spread_points(points_rows[0], row_spread)
-    row_tile = (first + pl.program_id(0)) * place[2] + place[0]
+def trail_kernel(
+    first,
+    place,
+    own,
+    gathered,
+    col_rows,
+    panel,
+    rows_0,
+    rows_1,
+    rows_2,
+    rows_3,
+    panel_in,
+    trail_in,
+    panel_out,
+    trail_out,
+    row_points,
+    col_points,
+    col_table,
+    row_spread,
+    rows,
+):
+    step = pl.program_id(0)
+    tile = row_points.shape[1]
+    _, groups, piece, _ = rows_0.shape
+
+    @pl.when(step == 0)
+    def _():
+        take_columns(gathered, pl.multiple_of(place[3] * tile, tile), col_points)
+        column_table(col_points, col_table)
+
+    take_slot(own, first + step, row_points)
+    spread_points(row_points, row_spread)
+    row_tile = (first + step) * place[2] + place[0]
+    mine = lax.rem(place[1], GROUP)
+    for which, source in enumerate((rows_0, rows_1, rows_2, rows_3)):
+        for group in range(groups):
+            begin = (group * GROUP + jnp.bitwise_xor(mine, which)) * piece
+            rows[pl.ds(pl.multiple_of(begin, piece), piece), :] = source[0, group]
+    panel_out[...] = panel[...]
     for part in row_parts(tile):
-        update = dot_nt(rows[0, part, :], col_rows[...])
+        update = dot_nt(rows[part, :], col_rows[...])
         for start in range(0, tile, 128):
             lanes = slice(start, start + 128)
             for row in range(part.start, part.stop, CHUNK):
@@ -511,29 +567,28 @@
     col_index = lax.axis_index("col")
     lead = PANELS * tile
     half_tile = tile // 2
-    shared = slots // SHARE
+    shared = slots * SHARED // SLOTS
     kept = slots - shared
+    groups = col_count // GROUP
     used = -(-(PANELS + col_count) // row_count)
     own = jnp.concatenate([grid_points, variable[None]], 0)
     gathered = lax.all_gather(own[:, :used], "row", axis=2, tiled=True).reshape(3, -1)
     target = PANELS + col_index
-    pad = lambda value: jnp.pad(value.astype(f32), ((0, 5), (0, 0)))
-    lead_points = pad(gathered[:, :lead])
     col_values = lax.dynamic_slice_in_dim(gathered, target * tile, tile, 1)
-    col_points = pad(col_values)
-    lead_table = column_table(gathered[2, :lead])
-    col_table = column_table(col_values[2])
-    points_rows = jnp.pad(jnp.transpose(own, (1, 0, 2)).astype(f32), ((0, 0), (0, 5), (0, 0)))
-    pieces = lax.dynamic_slice_in_dim(own[:, kept:], col_index * piece, piece, 2).reshape(3, shared * piece)
-    first_rows = jnp.concatenate([col_values, pieces], 1).astype(f32)
-    count = -(-first_rows.shape[1] // 128) * 128
-    first_rows = jnp.pad(first_rows, ((0, 5), (0, count - first_rows.shape[1])))
+    pieces = own[:, kept:].reshape(3, shared, groups, GROUP, piece)
+    pieces = lax.dynamic_index_in_dim(pieces, lax.rem(col_index, GROUP), 3, False).reshape(3, -1)
+    exact = tile + pieces.shape[1]
+    count = -(-exact // 128) * 128
+    first_rows = jnp.concatenate([col_values, pieces, jnp.zeros((3, count - exact), jnp.int32)], 1)
     place = jnp.stack([row_index, col_index, jnp.int32(row_count), target]).astype(jnp.int32)
-    whole = lambda shape: pl.BlockSpec(shape, lambda i, *s: (0,) * len(shape))
+    whole = lambda shape: pl.BlockSpec(shape, lambda i, s: (0,) * len(shape), pipeline_mode=pl.Buffered(1))
+    any_place = pl.BlockSpec(memory_space=pl.ANY)
     panel_shape = jax.ShapeDtypeStruct((slots, piece, lead), f32)
     trail_shape = jax.ShapeDtypeStruct((slots, tile, tile), f32)
     low_shape = (lead - tile, 2 * (lead - tile))
     diag_shape = (PANELS, half_tile, 9 * half_tile)
+    exchange_shape = (shared, groups, piece, lead)
+    points = lambda columns: [pltpu.VMEM((8, columns), f32), pltpu.VMEM((16, columns), f32)]
     layout = [
         pltpu.VMEM((lead - tile, 3 * (lead - tile)), bf16),
         pltpu.VMEM((PANELS, half_tile, 6 * half_tile), bf16),
@@ -545,41 +600,50 @@
         pltpu.VMEM((rows, 12 * half_tile), bf16),
         pltpu.VMEM((rows, 3 * lead), bf16),
     ]
-    params = pltpu.CompilerParams(dimension_semantics=("arbitrary",), vmem_limit_bytes=58 * 1024 * 1024)
+    params = pltpu.CompilerParams(dimension_semantics=("arbitrary",), vmem_limit_bytes=60 * 1024 * 1024)
     cost = lambda rows, size: pl.CostEstimate(flops=6 * rows * lead * lead, bytes_accessed=size, transcendentals=0)
-    panel, low, diag, col_rows, shared_rows = pl.pallas_call(
+    panel_part, low, diag, col_rows, shared_rows = pl.pallas_call(
         factor_kernel,
         out_shape=(
-            panel_shape,
+            jax.ShapeDtypeStruct((shared, piece, lead), f32),
             jax.ShapeDtypeStruct(low_shape, bf16),
             jax.ShapeDtypeStruct(diag_shape, bf16),
             jax.ShapeDtypeStruct((tile, lead), bf16),
-            jax.ShapeDtypeStruct((shared * piece, lead), bf16),
+            jax.ShapeDtypeStruct((exact - tile, lead), bf16),
         ),
-        grid=(1,),
-        in_specs=[whole((8, count)), whole((8, lead)), whole((16, lead))],
-        out_specs=(
-            pl.BlockSpec((shared, piece, lead), lambda i: (SHARE - 1, 0, 0)),
-            whole(low_shape),
-            whole(diag_shape),
-            whole((tile, lead)),
-            whole((shared * piece, lead)),
+        grid_spec=pltpu.PrefetchScalarGridSpec(
+            num_scalar_prefetch=1,
+            grid=(1,),
+            in_specs=[whole((3, count)), whole(gathered.shape)],
+            out_specs=(
+                whole((shared, piece, lead)),
+                whole(low_shape),
+                whole(diag_shape),
+                whole((tile, lead)),
+                whole((exact - tile, lead)),
+            ),
+            scratch_shapes=[pltpu.VMEM((8, count), f32)]
+            + points(lead)
+            + [pltpu.VMEM((lead, lead), f32), pltpu.VMEM((3, max(lead, count), 128), f32)]
+            + layout
+            + [
+                pltpu.VMEM((lead, half_tile), bf16),
+                pltpu.VMEM((lead, half_tile), bf16),
+                pltpu.VMEM((2, SUB, SUB), f32),
+                pltpu.VMEM((SUB, SUB), f32),
+                pltpu.VMEM((2, half_tile, half_tile), f32),
+                pltpu.VMEM((half_tile, half_tile), f32),
+            ]
+            + buffers(count)[2:],
         ),
-        scratch_shapes=[pltpu.VMEM((lead, lead), f32), pltpu.VMEM((3, lead, 128), f32)]
-        + layout
-        + [
-            pltpu.VMEM((lead, half_tile), bf16),
-            pltpu.VMEM((lead, half_tile), bf16),
-            pltpu.VMEM((2, SUB, SUB), f32),
-            pltpu.VMEM((SUB, SUB), f32),
-            pltpu.VMEM((2, half_tile, half_tile), f32),
-            pltpu.VMEM((half_tile, half_tile), f32),
-        ]
-        + buffers(count),
         compiler_params=params,
         cost_estimate=cost(count + lead, 20 * tile * lead),
-    )(first_rows, lead_points, lead_table)
-    panel_half = lax.all_gather(shared_rows.reshape(shared, piece, lead), "col", axis=1, tiled=True)
+    )(place, first_rows, gathered)
+    rows_0 = shared_rows.reshape(exchange_shape)
+    others = [
+        lax.ppermute(rows_0, "col", [(device, device ^ which) for device in range(col_count)])
+        for which in range(1, GROUP)
+    ]
     panel, trail = pl.pallas_call(
         rows_kernel,
         out_shape=(panel_shape, trail_shape),
@@ -587,49 +651,46 @@
             num_scalar_prefetch=1,
             grid=(kept,),
             in_specs=[
-                pl.BlockSpec((1, 8, tile), lambda i, s: (i, 0, 0)),
-                pl.BlockSpec((1, 8, tile), lambda i, s: (jnp.minimum(i + 1, kept - 1), 0, 0)),
-                whole((8, lead)),
-                whole((16, lead)),
-                whole((8, tile)),
-                whole((16, tile)),
+                whole(own.shape),
+                whole(gathered.shape),
                 whole(low_shape),
                 whole(diag_shape),
                 whole((tile, lead)),
-                pl.BlockSpec(memory_space=pl.ANY),
             ],
             out_specs=[
                 pl.BlockSpec((1, piece, lead), lambda i, s: (i, 0, 0)),
                 pl.BlockSpec((1, tile, tile), lambda i, s: (i, 0, 0)),
             ],
-            scratch_shapes=[pltpu.VMEM((3, tile, 128), f32)] + layout + buffers(tile),
+            scratch_shapes=[pltpu.VMEM((8, tile), f32)]
+            + points(lead)
+            + points(tile)
+            + [pltpu.VMEM((3, tile, 128), f32)]
+            + layout
+            + buffers(tile),
         ),
-        input_output_aliases={10: 0},
         compiler_params=params,
         cost_estimate=cost(kept * tile, 4 * kept * tile * (lead + tile)),
-    )(place, points_rows, points_rows, lead_points, lead_table, col_points, col_table, low, diag, col_rows, panel)
-    trail = pl.pallas_call(
+    )(place, own, gathered, low, diag, col_rows)
+    block = lambda shape: pl.BlockSpec((1,) + shape[1:], lambda i, s: (i,) + (0,) * (len(shape) - 1))
+    later = lambda shape: pl.BlockSpec((1,) + shape[1:], lambda i, s: (kept + i,) + (0,) * (len(shape) - 1))
+    return pl.pallas_call(
         functools.partial(trail_kernel, kept),
-        out_shape=trail_shape,
+        out_shape=(panel_shape, trail_shape),
         grid_spec=pltpu.PrefetchScalarGridSpec(
             num_scalar_prefetch=1,
             grid=(shared,),
-            in_specs=[
-                pl.BlockSpec((1, 8, tile), lambda i, s: (kept + i, 0, 0)),
-                whole((8, tile)),
-                whole((16, tile)),
-                pl.BlockSpec((1, tile, lead), lambda i, s: (i, 0, 0)),
-                whole((tile, lead)),
-                pl.BlockSpec(memory_space=pl.ANY),
-            ],
-            out_specs=pl.BlockSpec((1, tile, tile), lambda i, s: (kept + i, 0, 0)),
-            scratch_shapes=[pltpu.VMEM((3, tile, 128), f32)],
+            in_specs=[whole(own.shape), whole(gathered.shape), whole((tile, lead)), block(panel_part.shape)]
+            + [block(exchange_shape)] * GROUP
+            + [any_place, any_place],
+            out_specs=(later(panel_shape.shape), later(trail_shape.shape)),
+            scratch_shapes=[pltpu.VMEM((8, tile), f32)]
+            + points(tile)
+            + [pltpu.VMEM((3, tile, 128), f32), pltpu.VMEM((tile, lead), bf16)],
         ),
-        input_output_aliases={6: 0},
+        input_output_aliases={9: 0, 10: 1},
         compiler_params=params,
         cost_estimate=cost(shared * tile // 3, 4 * shared * tile * (lead + tile)),
-    )(place, points_rows, col_points, col_table, panel_half, col_rows, trail)
-    return panel, trail
+    )(place, own, gathered, col_rows, panel_part, rows_0, *others, panel, trail)
 
 
 def solution(mesh):

time: 234 us -> 228 us (0.974)
  between operations: 14.3 us -> 0.91 us
  Pallas kernels: 202 us -> 208 us
  local copies, waits for them, and re-layouts: 6.82 us -> 2.41 us
  starting transfers between devices: 0.04 us -> 3.58 us
    pallas_call x2, Pallas kernels: 98.8 us -> 116 us  [the longest x1 103 us: local(): pl.pallas_call(factor_kernel, out_shape=(jax.ShapeDtypeStruct((shared, pi...]
    pallas_call x1, Pallas kernels: 103 us -> 91.9 us  [local(): pl.pallas_call(rows_kernel, out_shape=(panel_shape, trail_shape), grid_sp...]
    ppermute x0 -> x3, starting transfers between devices: none -> 3.58 us  [local(): lax.ppermute(rows_0, 'col', [(device, device ^ which) for device in range...]
    another operation x2 -> x0, local copies, waits for them, and re-layouts: 2.64 us -> none  [column_table(): return jnp.stack(rows, 0)]
    pad x4 -> x0, local copies, waits for them, and re-layouts: 2.56 us -> none  [the longest x2 1.22 us: local(): pad = lambda value: jnp.pad(value.astype(f32), ((0, 5), (0, 0)))]
  transfers between devices with their start and end apart: 1 -> 3, of which waited for: 0 -> 0; matrix products, arithmetic and copies ran while one was open for 1% -> 0% of each run, Pallas kernels for 45% -> 41%
where the time goes in v4:
time: 228 us; the launch traced here: 225 us
  Pallas kernels  208 us (91%)
  blocking collectives  6.29 us (3%)
  starting transfers between devices  3.58 us (2%)
  other arithmetic  3.35 us (1%)
  local copies, waits for them, and re-layouts  2.41 us (1%)
    pallas_call x1, Pallas kernels, local(): pl.pallas_call(factor_kernel, out_shape=(jax.ShapeDtypeStruct((shared, pi...  103 us
    pallas_call x1, Pallas kernels, local(): pl.pallas_call(rows_kernel, out_shape=(panel_shape, trail_shape), grid_sp...  91.9 us
    pallas_call x1, Pallas kernels, local(): pl.pallas_call(functools.partial(trail_kernel, kept), out_shape=(panel_sh...  13.4 us
    all_gather x1, blocking collectives, local(): lax.all_gather(own[:, :used], 'row', axis=2, tiled=True).reshape(3, -1)  6.29 us
  transfers between devices with their start and end apart: 3, of which 0 were waited for; matrix products, arithmetic and copies ran while one was open for 0% of the time, Pallas kernels for 41%

profile of v4, /device:TPU:0, one launch (start us, length us, event | category | flops | bytes accessed | tf_op | source)
XLA Modules:
  0.0 224.8 jit_solution(4729314602762405736)
XLA Ops:
  0.6 0.8 copy.7
  1.4 0.7 fusion.1
  2.2 0.8 fusion
  3.0 0.1 reshape.18
  3.1 0.1 reshape.19
  3.2 6.3 %all_gather.3 = s32[3,3,2048]{2,1,0:T(4,128)S(1)} all-gather(s32[3,3,512]{2,1,0:T(4,128)S(1)} %fusion.1), channel_id=1, replica_groups=mesh['row'=4,'col'=8] {'row'}, dimensions={2}, use_global_device_ids=true | all-gather | bytes 92160 | tf_op jit(solution)/shard_map/all_gather | solution.py:575
  9.5 0.1 copy.10
  9.6 0.0 copy-start.1
  9.6 0.6 pad_add_fusion.1.first_rows
  10.2 0.6 pad_add_fusion.2.place
  10.8 0.0 copy-done.1
  10.8 0.0 copy-start
  10.8 102.9 %shard_map.41 = (f32[5,64,1536]{2,1,0:T(8,128)}, bf16[1024,2048]{1,0:T(8,128)(2,1)}, bf16[3,256,2304]{2,1,0:T(8,128)(2,1)}, bf16[512,1536]{1,0:T(8,128)(2,1)}, bf16[640,1536]{1,0:T(8,128)(2,1)}) custom-call(s32[4]{0:T(128)} %pad_add_fusion.2.place, s32[3,1152]{1,0:T(4,128)} %pad_add_fusion.1.first_rows, s32[3,6144]{1,0:T(4,128)} %bitcast.16), custom_call_target="tpu_custom_call" | custom-call | flops 38050725888 | bytes 15728640 | tf_op jit(solution)/shard_map/pallas_call | solution.py:605
  113.7 3.0 %collective-permute-start.2 = (bf16[5,2,64,1536]{3,2,1,0:T(8,128)(2,1)}, bf16[5,2,64,1536]{3,2,1,0:T(8,128)(2,1)S(1)}, u32[]{:S(2)}, u32[]{:S(2)}) collective-permute-start(bf16[5,2,64,1536]{3,2,1,0:T(8,128)(2,1)} %bitcast.19), channel_id=1, source_target_pairs={{0,3},{1,2},{2,1},{3,0},{4,7},{5,6},{6,5},{7,4},{8,11},{9,10},{10,... | collective-permute-start | bytes 5898248 | tf_op jit(solution)/shard_map/ppermute | solution.py:644
  116.7 0.5 collective-permute-start.1
  117.2 0.1 collective-permute-start
  117.3 0.0 copy-done
  117.3 0.6 pad_add_fusion.own
  118.0 91.9 %shard_map.42 = (f32[12,64,1536]{2,1,0:T(8,128)}, f32[12,512,512]{2,1,0:T(8,128)}) custom-call(s32[4]{0:T(128)} %pad_add_fusion.2.place, s32[3,12,512]{2,1,0:T(8,128)} %pad_add_fusion.own, s32[3,6144]{1,0:T(4,128)} %bitcast.17, bf16[1024,2048]{1,0:T(8,128)(2,1)} %get-tuple-element.12.low, bf16[3,256,2304]{2,1,0:T(8,128)(2,1)} %get-tuple-element.13.diag, ...), custom_call_target="tpu_custom_call" | custom-call | flops 50734301184 | bytes 29360128 | tf_op jit(solution)/shard_map/pallas_call | solution.py:647
  209.9 0.0 collective-permute-done.2.rows_3
  209.9 0.0 copy-start.2
  209.9 0.0 collective-permute-done.1.rows_2
  209.9 0.0 collective-permute-done.rows_1
  209.9 1.3 copy-done.2
  211.2 13.4 %shard_map.43 = (f32[12,64,1536]{2,1,0:T(8,128)}, f32[12,512,512]{2,1,0:T(8,128)}) custom-call(s32[4]{0:T(128)} %pad_add_fusion.2.place, s32[3,12,512]{2,1,0:T(8,128)} %pad_add_fusion.own, s32[3,6144]{1,0:T(4,128)} %bitcast.18, bf16[512,1536]{1,0:T(8,128)(2,1)} %get-tuple-element.9.col_rows, ...), custom_call_target="tpu_custom_call", output_to_operand_aliasing={{0}: (9, {}), {1}: (10, {})} | custom-call | flops 12074876928 | bytes 20971520 | tf_op jit(solution)/shard_map/pallas_call | solution.py:676
  (4 shorter events, 0.1 us)
Async XLA Ops:
  9.6 1.3 copy-start.1
  10.8 106.5 %copy-start = (s32[12,512]{1,0:T(8,128)S(1)}, s32[12,512]{1,0:T(8,128)}, u32[]{:S(2)}) copy-start(s32[12,512]{1,0:T(8,128)} %param.3) | copy-start | bytes 73732
  113.7 96.2 %collective-permute-start.2 = (bf16[5,2,64,1536]{3,2,1,0:T(8,128)(2,1)}, bf16[5,2,64,1536]{3,2,1,0:T(8,128)(2,1)S(1)}, u32[]{:S(2)}, u32[]{:S(2)}) collective-permute-start(bf16[5,2,64,1536]{3,2,1,0:T(8,128)(2,1)} %bitcast.19), channel_id=1, source_target_pairs={{0,3},{1,2},{2,1},{3,0},{4,7},{5,6},{6,5},{7,4},{8,11},{9,10},{10,... | collective-permute-start | bytes 5898248 | tf_op jit(solution)/shard_map/ppermute | solution.py:644
  116.7 93.2 %collective-permute-start.1 = (bf16[5,2,64,1536]{3,2,1,0:T(8,128)(2,1)}, bf16[5,2,64,1536]{3,2,1,0:T(8,128)(2,1)}, u32[]{:S(2)}, u32[]{:S(2)}) collective-permute-start(bf16[5,2,64,1536]{3,2,1,0:T(8,128)(2,1)} %bitcast.20), channel_id=1, source_target_pairs={{0,2},{1,3},{2,0},{3,1},{4,6},{5,7},{6,4},{7,5},{8,10},{9,11},{10,... | collective-permute-start | bytes 5898248 | tf_op jit(solution)/shard_map/ppermute | solution.py:644
  117.2 92.7 %collective-permute-start = (bf16[5,2,64,1536]{3,2,1,0:T(8,128)(2,1)}, bf16[5,2,64,1536]{3,2,1,0:T(8,128)(2,1)}, u32[]{:S(2)}, u32[]{:S(2)}) collective-permute-start(bf16[5,2,64,1536]{3,2,1,0:T(8,128)(2,1)} %bitcast.21), channel_id=1, source_target_pairs={{0,1},{1,0},{2,3},{3,2},{4,5},{5,4},{6,7},{7,6},{8,9},{9,8},{10,11... | collective-permute-start | bytes 5898248 | tf_op jit(solution)/shard_map/ppermute | solution.py:644
  209.9 1.3 copy-start.2

commit v5 on v4

--- a/solution.py
+++ b/solution.py
@@ -217,12 +217,12 @@
     panels, half_tile, _ = diag_first.shape
     tile = 2 * half_tile
     parts = row_parts(cov.shape[0])
-    portion = 0.25 / len(parts)
+    portion = 1.0 / (len(parts) * (12 * t + 18))
     for part in parts:
         known = None
         if t:
             known = dot_nt(rows_pieces[part, 0 : 3 * tile * t], low_pieces[tile * (t - 1) : tile * t, 0 : 3 * tile * t])
-        ahead.share(portion)
+        ahead.share(12 * t * portion)
         for start in range(0, tile, 128):
             lanes = slice(start, start + 128)
             for row in range(part.start, part.stop, CHUNK):
@@ -231,14 +231,18 @@
                 if t:
                     value = value - known[row - part.start : row - part.start + CHUNK, lanes]
                 pieces = split_three(value)
-                at = start if start < half_tile else start + 5 * half_tile
-                for order, kind in enumerate((0, 0, 0, 1, 1, 2)):
-                    residual[rows, at + half_tile * order : at + half_tile * order + 128] = pieces[kind]
-        ahead.share(portion)
+                at = start if start < half_tile else start + 2 * half_tile
+                for kind in range(3):
+                    residual[rows, at + half_tile * kind : at + half_tile * kind + 128] = pieces[kind]
     for part in parts:
         for half, diag in enumerate((diag_first, diag_second)):
-            solved = dot_nt(residual[part, 0 : 6 * half_tile * (half + 1)], diag[t])
-            ahead.share(portion)
+            left = [
+                residual[part, half_tile * (3 * group + kind) : half_tile * (3 * group + kind + 1)]
+                for group in range(half + 1)
+                for kind in (0, 0, 0, 1, 1, 2)
+            ]
+            solved = dot_nt(jnp.concatenate(left, 1), diag[t])
+            ahead.share(6 * (half + 1) * portion)
             high, rest = split_two(solved)
             at = 3 * tile * t + half_tile * half
             rows_pieces[part, at : at + half_tile] = high
@@ -276,6 +280,7 @@
     sub_lower,
     block_inverse,
     block_lower,
+    sub_product,
     residual,
     rows_pieces,
 ):
@@ -307,6 +312,7 @@
     def factor_step(b, _):
         base = pl.multiple_of(b * SUB, SUB)
         here = pl.ds(base, SUB)
+        sub_product[...] = dot_full(sub_lower[...], sub_inverse[0], ((1,), (0,)))
         result = inverse_factor([matrix[pl.ds(base + 8 * i, 8), here] for i in range(SUB // 8)])
         half = lax.rem(b, 2)
         for i in range(SUB // 8):
@@ -323,11 +329,7 @@
         def _():
             block = b // 2
             parity = lax.rem(block, 2)
-            corner = -dot_full(
-                sub_inverse[1],
-                dot_full(sub_lower[...], sub_inverse[0], ((1,), (0,))),
-                ((1,), (0,)),
-            )
+            corner = -dot_full(sub_inverse[1], sub_product[...], ((1,), (0,)))
             inverse = jnp.concatenate(
                 [
                     jnp.concatenate([sub_inverse[0], jnp.zeros((SUB, SUB), f32)], 1),
@@ -346,17 +348,21 @@
                     panel, odd = which // 2, which % 2
                     if begin < lead:
                         below_high, below_rest = split_two(matrix[begin:, here])
-                        solved = dot_nt(below_high, high) + dot_nt(below_high, mid) + dot_nt(below_rest, high)
+                        solved = dot_nt(
+                            jnp.concatenate([below_high, below_high, below_rest], 1),
+                            jnp.concatenate([high, mid, high], 1),
+                        )
                         solved_high, solved_rest = split_two(solved)
                         step_high[begin:, :] = solved_high
                         step_rest[begin:, :] = solved_rest
                         for j in range(which + 1, blocks):
                             stripe = slice(half_tile * j, half_tile * (j + 1))
                             from_row = half_tile * j
-                            matrix[from_row:, stripe] = matrix[from_row:, stripe] - (
-                                dot_nt(step_high[from_row:, :], step_high[stripe, :])
-                                + dot_nt(step_high[from_row:, :], step_rest[stripe, :])
-                                + dot_nt(step_rest[from_row:, :], step_high[stripe, :])
+                            left_high, left_rest = step_high[from_row:, :], step_rest[from_row:, :]
+                            right_high, right_rest = step_high[stripe, :], step_rest[stripe, :]
+                            matrix[from_row:, stripe] = matrix[from_row:, stripe] - dot_nt(
+                                jnp.concatenate([left_high, left_high, left_rest], 1),
+                                jnp.concatenate([right_high, right_rest, right_high], 1),
                             )
                         if panel + 1 < panels:
                             later = slice(tile * (panel + 1), lead)
@@ -493,11 +499,12 @@
             panel_out[0, :, tile * t : tile * (t + 1)] = high + rest
         parts = row_parts(tile)
         for part in parts:
-            update = None
-            for t in range(panels):
-                at = 3 * tile * t
-                term = dot_nt(rows_pieces[part, at : at + tile], col_rows[:, tile * t : tile * (t + 1)])
-                update = term if update is None else update + term
+            update = dot_nt(
+                jnp.concatenate(
+                    [rows_pieces[part, 3 * tile * t : 3 * tile * t + tile] for t in range(panels)], 1
+                ),
+                col_rows[...],
+            )
             ahead.share(0.5 / len(parts))
             trail_out[0, part, :] = last[part, :] - update
             ahead.share(0.5 / len(parts))
@@ -597,7 +604,7 @@
     buffers = lambda rows: [
         pltpu.VMEM((rows, tile), f32),
         pltpu.VMEM((rows, tile), f32),
-        pltpu.VMEM((rows, 12 * half_tile), bf16),
+        pltpu.VMEM((rows, 6 * half_tile), bf16),
         pltpu.VMEM((rows, 3 * lead), bf16),
     ]
     params = pltpu.CompilerParams(dimension_semantics=("arbitrary",), vmem_limit_bytes=60 * 1024 * 1024)
@@ -633,6 +640,7 @@
                 pltpu.VMEM((SUB, SUB), f32),
                 pltpu.VMEM((2, half_tile, half_tile), f32),
                 pltpu.VMEM((half_tile, half_tile), f32),
+                pltpu.VMEM((SUB, SUB), f32),
             ]
             + buffers(count)[2:],
         ),

time: 228 us -> 224 us (0.982)
  Pallas kernels: 208 us -> 204 us
    pallas_call x1, Pallas kernels: 91.9 us -> 89.6 us  [local(): pl.pallas_call(rows_kernel, out_shape=(panel_shape, trail_shape), grid_sp...]
where the time goes in v5:
time: 224 us; the launch traced here: 221 us
  Pallas kernels  204 us (91%)
  blocking collectives  6.29 us (3%)
  starting transfers between devices  3.58 us (2%)
  other arithmetic  3.35 us (1%)
  local copies, waits for them, and re-layouts  2.41 us (1%)
    pallas_call x1, Pallas kernels, local(): pl.pallas_call(factor_kernel, out_shape=(jax.ShapeDtypeStruct((shared, pi...  101 us
    pallas_call x1, Pallas kernels, local(): pl.pallas_call(rows_kernel, out_shape=(panel_shape, trail_shape), grid_sp...  89.6 us
    pallas_call x1, Pallas kernels, local(): pl.pallas_call(functools.partial(trail_kernel, kept), out_shape=(panel_sh...  13.4 us
    all_gather x1, blocking collectives, local(): lax.all_gather(own[:, :used], 'row', axis=2, tiled=True).reshape(3, -1)  6.29 us
  transfers between devices with their start and end apart: 3, of which 0 were waited for; matrix products, arithmetic and copies ran while one was open for 0% of the time, Pallas kernels for 41%

profile of v5, /device:TPU:0, one launch (start us, length us, event | category | flops | bytes accessed | tf_op | source)
XLA Modules:
  0.0 220.8 jit_solution(584522140370322468)
XLA Ops:
  0.6 0.8 copy.7
  1.4 0.7 fusion.1
  2.2 0.8 fusion
  3.0 0.1 reshape.18
  3.1 0.1 reshape.19
  3.2 6.3 %all_gather.3 = s32[3,3,2048]{2,1,0:T(4,128)S(1)} all-gather(s32[3,3,512]{2,1,0:T(4,128)S(1)} %fusion.1), channel_id=1, replica_groups=mesh['row'=4,'col'=8] {'row'}, dimensions={2}, use_global_device_ids=true | all-gather | bytes 92160 | tf_op jit(solution)/shard_map/all_gather | solution.py:582
  9.5 0.1 copy.10
  9.6 0.0 copy-start.1
  9.6 0.6 pad_add_fusion.1.first_rows
  10.2 0.6 pad_add_fusion.2.place
  10.8 0.0 copy-done.1
  10.8 0.0 copy-start
  10.8 101.2 %shard_map.41 = (f32[5,64,1536]{2,1,0:T(8,128)}, bf16[1024,2048]{1,0:T(8,128)(2,1)}, bf16[3,256,2304]{2,1,0:T(8,128)(2,1)}, bf16[512,1536]{1,0:T(8,128)(2,1)}, bf16[640,1536]{1,0:T(8,128)(2,1)}) custom-call(s32[4]{0:T(128)} %pad_add_fusion.2.place, s32[3,1152]{1,0:T(4,128)} %pad_add_fusion.1.first_rows, s32[3,6144]{1,0:T(4,128)} %bitcast.16), custom_call_target="tpu_custom_call" | custom-call | flops 38050725888 | bytes 15728640 | tf_op jit(solution)/shard_map/pallas_call | solution.py:612
  112.0 3.0 %collective-permute-start.2 = (bf16[5,2,64,1536]{3,2,1,0:T(8,128)(2,1)}, bf16[5,2,64,1536]{3,2,1,0:T(8,128)(2,1)S(1)}, u32[]{:S(2)}, u32[]{:S(2)}) collective-permute-start(bf16[5,2,64,1536]{3,2,1,0:T(8,128)(2,1)} %bitcast.19), channel_id=1, source_target_pairs={{0,3},{1,2},{2,1},{3,0},{4,7},{5,6},{6,5},{7,4},{8,11},{9,10},{10,... | collective-permute-start | bytes 5898248 | tf_op jit(solution)/shard_map/ppermute | solution.py:652
  115.0 0.4 collective-permute-start.1
  115.5 0.1 collective-permute-start
  115.6 0.0 copy-done
  115.6 0.6 pad_add_fusion.own
  116.2 89.6 %shard_map.42 = (f32[12,64,1536]{2,1,0:T(8,128)}, f32[12,512,512]{2,1,0:T(8,128)}) custom-call(s32[4]{0:T(128)} %pad_add_fusion.2.place, s32[3,12,512]{2,1,0:T(8,128)} %pad_add_fusion.own, s32[3,6144]{1,0:T(4,128)} %bitcast.17, bf16[1024,2048]{1,0:T(8,128)(2,1)} %get-tuple-element.12.low, bf16[3,256,2304]{2,1,0:T(8,128)(2,1)} %get-tuple-element.13.diag, ...), custom_call_target="tpu_custom_call" | custom-call | flops 50734301184 | bytes 29360128 | tf_op jit(solution)/shard_map/pallas_call | solution.py:655
  205.8 0.0 collective-permute-done.2.rows_3
  205.8 0.0 copy-start.2
  205.8 0.0 collective-permute-done.1.rows_2
  205.8 0.0 collective-permute-done.rows_1
  205.8 1.3 copy-done.2
  207.1 13.4 %shard_map.43 = (f32[12,64,1536]{2,1,0:T(8,128)}, f32[12,512,512]{2,1,0:T(8,128)}) custom-call(s32[4]{0:T(128)} %pad_add_fusion.2.place, s32[3,12,512]{2,1,0:T(8,128)} %pad_add_fusion.own, s32[3,6144]{1,0:T(4,128)} %bitcast.18, bf16[512,1536]{1,0:T(8,128)(2,1)} %get-tuple-element.9.col_rows, ...), custom_call_target="tpu_custom_call", output_to_operand_aliasing={{0}: (9, {}), {1}: (10, {})} | custom-call | flops 12074876928 | bytes 20971520 | tf_op jit(solution)/shard_map/pallas_call | solution.py:684
  (4 shorter events, 0.1 us)
Async XLA Ops:
  9.6 1.3 copy-start.1
  10.8 104.8 %copy-start = (s32[12,512]{1,0:T(8,128)S(1)}, s32[12,512]{1,0:T(8,128)}, u32[]{:S(2)}) copy-start(s32[12,512]{1,0:T(8,128)} %param.3) | copy-start | bytes 73732
  112.0 93.8 %collective-permute-start.2 = (bf16[5,2,64,1536]{3,2,1,0:T(8,128)(2,1)}, bf16[5,2,64,1536]{3,2,1,0:T(8,128)(2,1)S(1)}, u32[]{:S(2)}, u32[]{:S(2)}) collective-permute-start(bf16[5,2,64,1536]{3,2,1,0:T(8,128)(2,1)} %bitcast.19), channel_id=1, source_target_pairs={{0,3},{1,2},{2,1},{3,0},{4,7},{5,6},{6,5},{7,4},{8,11},{9,10},{10,... | collective-permute-start | bytes 5898248 | tf_op jit(solution)/shard_map/ppermute | solution.py:652
  115.0 90.8 %collective-permute-start.1 = (bf16[5,2,64,1536]{3,2,1,0:T(8,128)(2,1)}, bf16[5,2,64,1536]{3,2,1,0:T(8,128)(2,1)}, u32[]{:S(2)}, u32[]{:S(2)}) collective-permute-start(bf16[5,2,64,1536]{3,2,1,0:T(8,128)(2,1)} %bitcast.20), channel_id=1, source_target_pairs={{0,2},{1,3},{2,0},{3,1},{4,6},{5,7},{6,4},{7,5},{8,10},{9,11},{10,... | collective-permute-start | bytes 5898248 | tf_op jit(solution)/shard_map/ppermute | solution.py:652
  115.5 90.4 %collective-permute-start = (bf16[5,2,64,1536]{3,2,1,0:T(8,128)(2,1)}, bf16[5,2,64,1536]{3,2,1,0:T(8,128)(2,1)}, u32[]{:S(2)}, u32[]{:S(2)}) collective-permute-start(bf16[5,2,64,1536]{3,2,1,0:T(8,128)(2,1)} %bitcast.21), channel_id=1, source_target_pairs={{0,1},{1,0},{2,3},{3,2},{4,5},{5,4},{6,7},{7,6},{8,9},{9,8},{10,11... | collective-permute-start | bytes 5898248 | tf_op jit(solution)/shard_map/ppermute | solution.py:652
  205.8 1.3 copy-start.2
